TPU v7x, 128 devices: a whole 4x4x4 slice. The times are simulated.
128 devices in a mesh: ctx: 64 (over x, z, y), tp: 2 (over core).
Axes of the slice: x: 4, y: 4, z: 4, core: 2. Of those that a mesh axis runs over, the one named last changes fastest.
Arguments:
- inputs: bfloat16 [32768, 4, 1024], P('ctx', None, 'tp'), may hold values from -6 to 6
- grad_out: bfloat16 [32768, 4, 1024], P('ctx', None, 'tp'), may hold values from -6 to 6
- dt_raw: float32 [4, 16, 32768], P(None, 'tp', 'ctx'), may hold values from -14 to 0
- dt_bias: float32 [4, 16], P(None, 'tp'), may hold values from -0.5 to 0.5
- a_log: float32 [4, 16], P(None, 'tp'), may hold values from -0.5 to 0.5
- b_proj: bfloat16 [32768, 4, 64], P('ctx'), may hold values from -2 to 2
- c_proj: bfloat16 [32768, 4, 64], P('ctx'), may hold values from -2 to 2
Outputs:
- grad_inputs: bfloat16 [32768, 4, 1024], P('ctx', None, 'tp')
- grad_raw: float32 [4, 16, 32768], P(None, 'tp', 'ctx')
- grad_alog: float32 [4, 16], P(None, 'tp')
- grad_bias: float32 [4, 16], P(None, 'tp')
- grad_b: bfloat16 [32768, 4, 64], P('ctx', 'tp')
- grad_c: bfloat16 [32768, 4, 64], P('ctx', 'tp')
All inputs are finite; a program needn't handle non-finite values.
Results may differ from a plain program's by a relative error of at most 0.011.
Values may be sent and summed in bfloat16 or wider, within the bound.
A program may use at most 448 MiB of HBM per device.

v0:
```python
import jax
import jax.numpy as jnp
from jax import lax
from jax.sharding import PartitionSpec as P

HIGHEST = lax.Precision.HIGHEST


def prefix(value, axis, join, neutral, backward):
    count, mine = (lax.axis_size(axis), lax.axis_index(axis))
    pieces = jax.tree.map(lambda part: lax.all_gather(part, axis), value)
    if backward:
        pieces = jax.tree.map(lambda part: part[::-1], pieces)
        mine = count - 1 - mine
    total = jax.tree.map(
        lambda part, zero: jnp.full_like(part, 0) + jnp.asarray(zero, part.dtype), value, neutral
    )

    def lap(position, total):
        longer = join(total, jax.tree.map(lambda part: part[position], pieces))
        return jax.tree.map(lambda new, old: jnp.where(position < mine, new, old), longer, total)

    return lax.fori_loop(0, count - 1, lap, total)


def lower_table(length):
    order = jnp.arange(length)
    return (order[:, None] >= order[None, :]).astype(jnp.float32)


def decays_of(raw_rates, dt_bias, a_log):
    time_step_width = jax.nn.softplus(raw_rates + dt_bias[:, :, None])
    rates = jnp.exp(a_log)
    log_decay = -time_step_width * rates[:, :, None]
    cumulative = jnp.einsum(
        "ghm,lm->ghl", log_decay, lower_table(raw_rates.shape[2]), precision=HIGHEST
    )
    return (time_step_width, rates, cumulative)


def weighted(inputs4, grad4, time_step_width, cumulative):
    final = cumulative[:, :, -1:]
    end_weight = jnp.exp(final - cumulative) * time_step_width
    start_weight = jnp.exp(cumulative)
    scaled_input = (inputs4 * jnp.transpose(end_weight, (2, 0, 1))[..., None]).astype(jnp.bfloat16)
    scaled_grad = (grad4 * jnp.transpose(start_weight, (2, 0, 1))[..., None]).astype(jnp.bfloat16)
    return (scaled_input, scaled_grad, start_weight)


def split_heads(inputs, grad_out, raw_rates):
    length, groups, width = inputs.shape
    heads = raw_rates.shape[1]
    inputs4 = inputs.reshape(length, groups, heads, width // heads)
    grad4 = grad_out.reshape(length, groups, heads, width // heads)
    return (inputs4, grad4)


def within_block(inputs_g, grad_g, b_g, c_g, cumulative, time_step_width):
    length = inputs_g.shape[0]
    order = jnp.arange(length)
    lower = order[:, None] >= order[None, :]
    intersection = jnp.einsum("ln,mn->lm", c_g, b_g, preferred_element_type=jnp.float32)
    spread = jnp.where(lower, cumulative[:, :, None] - cumulative[:, None, :], 0.0)
    decay_mat = jnp.where(lower, jnp.exp(spread), 0.0)
    pair = jnp.einsum("lhp,mhp->hlm", grad_g, inputs_g, preferred_element_type=jnp.float32)
    mixing = (decay_mat * intersection).astype(jnp.bfloat16)
    grad_state = jnp.einsum("hlm,lhp->mhp", mixing, grad_g, preferred_element_type=jnp.float32)
    weights = decay_mat * pair * time_step_width[:, None, :]
    weights_low = weights.astype(jnp.bfloat16)
    grad_c = jnp.einsum("hlm,mn->ln", weights_low, b_g, preferred_element_type=jnp.float32)
    grad_b = jnp.einsum("hlm,ln->mn", weights_low, c_g, preferred_element_type=jnp.float32)
    terms = weights * intersection
    balance = jnp.sum(terms, axis=2) - jnp.sum(terms, axis=1)
    return (grad_state, grad_b, grad_c, balance)


def combine(earlier, later):
    return (earlier[0] * later[0], later[0][:, :, None, None] * earlier[1] + later[1])


def layer_grads(inputs, grad_out, raw_rates, dt_bias, a_log, b_blk, c_blk):
    length, groups, width = inputs.shape
    inputs4, grad4 = split_heads(inputs, grad_out, raw_rates)
    time_step_width, rates, cumulative = decays_of(raw_rates, dt_bias, a_log)
    scaled_input, scaled_grad, start_weight = weighted(inputs4, grad4, time_step_width, cumulative)
    final = cumulative[:, :, -1]
    decay = jnp.exp(final)
    ends = jnp.einsum("lghp,lgn->ghpn", scaled_input, b_blk, preferred_element_type=jnp.float32)
    starts = jnp.einsum("lghp,lgn->ghpn", scaled_grad, c_blk, preferred_element_type=jnp.float32)
    unit = (jnp.ones_like(decay), jnp.zeros_like(ends))
    states_in = prefix((decay, ends), "ctx", combine, unit, False)[1]
    grads_in = prefix((decay, starts), "ctx", combine, unit, True)[1]
    state_low = states_in.astype(jnp.bfloat16)
    grad_low = grads_in.astype(jnp.bfloat16)
    tail_weight = jnp.transpose(jnp.exp(final[:, :, None] - cumulative), (2, 0, 1))[..., None]
    cross_grad = (
        jnp.einsum("lgn,ghpn->lghp", b_blk, grad_low, preferred_element_type=jnp.float32)
        * tail_weight
    )
    cross_out = (
        jnp.einsum("lgn,ghpn->lghp", c_blk, state_low, preferred_element_type=jnp.float32)
        * jnp.transpose(start_weight, (2, 0, 1))[..., None]
    )
    cross_b = jnp.einsum(
        "lghp,ghpn->lgn", scaled_input, grad_low, preferred_element_type=jnp.float32
    )
    cross_c = jnp.einsum(
        "lghp,ghpn->lgn", scaled_grad, state_low, preferred_element_type=jnp.float32
    )
    parts = lax.map(
        lambda item: within_block(*item),
        (
            jnp.moveaxis(inputs4, 1, 0),
            jnp.moveaxis(grad4, 1, 0),
            jnp.moveaxis(b_blk, 1, 0),
            jnp.moveaxis(c_blk, 1, 0),
            cumulative,
            time_step_width,
        ),
    )
    grad_state = jnp.moveaxis(parts[0], 0, 1) + cross_grad
    step_rows = jnp.transpose(time_step_width, (2, 0, 1))
    grad_inputs = (
        (step_rows[..., None] * grad_state).astype(jnp.bfloat16).reshape(length, groups, width)
    )
    along = jnp.transpose(jnp.sum(inputs4 * grad_state, axis=3), (1, 2, 0))
    inflow = jnp.transpose(jnp.sum(grad4 * cross_out, axis=3), (1, 2, 0))
    outflow = time_step_width * jnp.transpose(jnp.sum(inputs4 * cross_grad, axis=3), (1, 2, 0))
    through = decay * jnp.sum(grads_in * states_in, axis=(2, 3))
    balance = parts[3] + inflow - outflow
    suffix = jnp.einsum("ghj,ju->ghu", balance, lower_table(length), precision=HIGHEST)
    log_grad = suffix + jnp.sum(outflow, axis=2, keepdims=True) + through[:, :, None]
    grad_step = along - rates[:, :, None] * log_grad
    grad_raw = grad_step * jax.nn.sigmoid(raw_rates + dt_bias[:, :, None])
    grad_alog = jnp.sum(log_grad * (-time_step_width * rates[:, :, None]), axis=2)
    grad_bias = jnp.sum(grad_raw, axis=2)
    grad_b = jnp.moveaxis(parts[1], 0, 1) + cross_b
    grad_c = jnp.moveaxis(parts[2], 0, 1) + cross_c
    return (grad_inputs, grad_raw, grad_alog, grad_bias, grad_b, grad_c)


def body(inputs, grad_out, dt_raw, dt_bias, a_log, b_proj, c_proj):
    grad_inputs, grad_raw, alog_term, bias_term, b_part, c_part = layer_grads(
        inputs, grad_out, dt_raw, dt_bias, a_log, b_proj, c_proj
    )
    b_sum, c_sum = (
        lax.psum_scatter(b_part, "tp", scatter_dimension=1, tiled=True),
        lax.psum_scatter(c_part, "tp", scatter_dimension=1, tiled=True),
    )
    grad_b = b_sum.astype(jnp.bfloat16)
    grad_c = c_sum.astype(jnp.bfloat16)
    grad_alog, grad_bias = lax.psum((alog_term, bias_term), "ctx")
    return (grad_inputs, grad_raw, grad_alog, grad_bias, grad_b, grad_c)


def solution(mesh):
    in_specs = (
        P("ctx", None, "tp"),
        P("ctx", None, "tp"),
        P(None, "tp", "ctx"),
        P(None, "tp"),
        P(None, "tp"),
        P("ctx", None, None),
        P("ctx", None, None),
    )
    out_specs = (
        P("ctx", None, "tp"),
        P(None, "tp", "ctx"),
        P(None, "tp"),
        P(None, "tp"),
        P("ctx", "tp", None),
        P("ctx", "tp", None),
    )
    return jax.shard_map(body, mesh=mesh, in_specs=in_specs, out_specs=out_specs, check_vma=False)
```

profile of v0, /device:TPU:0, one launch (start us, length us, event | category | flops | bytes accessed | tf_op | source)
XLA Modules:
  0.0 914.7 jit_solution(17345953553483891700)
XLA Ops:
  9.6 1.6 multiply_bitcast_fusion
  11.2 3.0 copy.38
  14.2 1.7 fusion.41
  16.1 3.0 copy.41
  19.1 1.7 fusion.37
  21.5 190.7 %all-gather = f32[256,8,1]{1,2,0:T(1,128)} all-gather(f32[4,8,1]{1,2,0:T(1,128)S(1)} %bitcast.232), channel_id=2, replica_groups=mesh['ctx'=64,'tp'=2] {'ctx'}, dimensions={0}, use_global_device_ids=true | all-gather | bytes 8320 | tf_op jit(solution)/shard_map/all_gather | solution.py:11
  212.2 1.6 rev.6
  214.6 58.5 %while.47 = (s32[]{:T(128)}, f32[4,512,8,64]{1,3,2,0:T(8,128)}, f32[4,512,64]{1,2,0:T(8,128)}, f32[4,512,64]{1,2,0:T(8,128)}, f32[4,8,512]{2,1,0:T(8,128)}, /*in...) while((s32[]{:T(128)}, f32[4,512,8,64]{1,3,2,0:T(8,128)}, ...), condition=%wide.region_4.5_spmd.clone, body=%wide.region_0.4_spmd.sunk.clone | while | flops 671084544 | bytes 9148017 | solution.py:110
  215.7 5.0 fusion.117
  220.6 6.1 multiply_reduce_fusion.6
  230.3 5.0 fusion.117
  235.3 6.1 multiply_reduce_fusion.6
  244.9 5.0 fusion.117
  249.9 6.1 multiply_reduce_fusion.6
  259.6 5.0 fusion.117
  264.5 6.1 multiply_reduce_fusion.6
  273.1 23.3 %all-gather.6.cloned.1.call-done = f32[256,8,64,64]{3,2,1,0:T(8,128)} async-done(((f32[4,8,64,64]{3,2,1,0:T(8,128)}), f32[256,8,64,64]{3,2,1,0:T(8,128)}) %all-gather.6.cloned.1.call-update) | async-done | bytes 33554448 | tf_op jit(solution)/shard_map/all_gather | solution.py:11
  296.3 45.3 %rev.7 = f32[64,4,8,64,64]{4,3,2,1,0:T(8,128)} reverse(f32[64,4,8,64,64]{4,3,2,1,0:T(8,128)} %bitcast.25), dimensions={0} | reverse | bytes 67108864 | tf_op jit(solution)/shard_map/rev | solution.py:13
  341.6 139.0 %while.48 = (s32[]{:T(128)}, f32[4,8,64,64]{3,2,1,0:T(8,128)S(1)}, s32[]{:T(128)}, f32[64,4,8]{2,1,0:T(4,128)}, f32[64,4,8,64,64]{4,3,2,1,0:T(8,128)}) while((s32[]{:T(128)}, f32[4,8,64,64]{3,2,1,0:T(8,128)S(1)}, s32[]{:T(128)}, f32[64,4,8]{2,1,0:T(4,128)}, f32[64,4,8,64,64]{4,3,2,1,0:T(8,128)}) %tuple.107), condition=%wide.region_6.7_spmd.clone.clone, body=%wide.region_5.6_spmd.clone.sunk.clone | while | flops 524292 | bytes 1573337 | solution.py:23
  342.4 1.5 fusion.120
  344.6 1.5 fusion.120
  346.8 1.5 fusion.120
  349.0 1.5 fusion.120
  351.2 1.5 fusion.120
  353.4 1.5 fusion.120
  357.8 1.5 fusion.120
  360.0 1.5 fusion.120
  362.2 1.5 fusion.120
  364.4 1.5 fusion.120
  368.8 1.5 fusion.120
  375.3 1.5 fusion.120
  384.0 1.5 fusion.120
  390.5 1.8 fusion.120
  393.0 1.8 fusion.120
  395.5 1.8 fusion.120
  410.9 1.5 fusion.120
  413.2 1.5 fusion.120
  415.4 1.5 fusion.120
  426.3 1.5 fusion.120
  428.5 1.5 fusion.120
  430.8 1.5 fusion.120
  441.7 1.5 fusion.120
  443.9 1.5 fusion.120
  446.1 1.5 fusion.120
  454.9 1.5 fusion.120
  457.1 1.5 fusion.120
  459.3 1.5 fusion.120
  461.6 1.5 fusion.120
  470.3 1.5 fusion.120
  472.5 1.5 fusion.120
  474.8 1.5 fusion.120
  477.0 1.5 fusion.120
  480.7 3.0 fusion.49
  484.0 91.0 %all-gather.8.cloned.1.call-done = f32[256,8,64,64]{3,2,1,0:T(8,128)} async-done(((f32[4,8,64,64]{3,2,1,0:T(8,128)}), f32[256,8,64,64]{3,2,1,0:T(8,128)}) %all-gather.8.cloned.1.call-update) | async-done | bytes 33554448 | tf_op jit(solution)/shard_map/all_gather | solution.py:11
  575.0 135.4 %while.49 = (s32[]{:T(128)}, f32[4,8,64,64]{3,2,1,0:T(8,128)S(1)}, s32[]{:T(128)}, f32[64,4,8]{2,1,0:T(4,128)}, f32[64,4,8,64,64]{4,3,2,1,0:T(8,128)}) while((s32[]{:T(128)}, f32[4,8,64,64]{3,2,1,0:T(8,128)S(1)}, s32[]{:T(128)}, f32[64,4,8]{2,1,0:T(4,128)}, f32[64,4,8,64,64]{4,3,2,1,0:T(8,128)}) %tuple.125), condition=%wide.region_9.10_spmd.clone.clone, body=%wide.region_8.9_spmd.clone.sunk.clone | while | flops 524292 | bytes 1573337 | solution.py:23
  584.3 1.5 fusion.121
  586.4 1.5 fusion.121
  710.4 3.1 fusion.52
  713.5 5.7 fusion.34
  719.5 4.6 copy.46
  724.0 2.4 fusion.31
  727.6 177.3 %all-reduce = (f32[4,8]{1,0:T(4,128)}, f32[4,8]{1,0:T(4,128)}) all-reduce(f32[4,8]{1,0:T(4,128)S(1)} %get-tuple-element.374, f32[4,8]{1,0:T(4,128)S(1)} %get-tuple-element.369), channel_id=1, replica_groups=mesh['ctx'=64,'tp'=2] {'ctx'}, use_global_device_ids=true, to_apply=%region_15.16 | all-reduce | flops 64 | bytes 512 | tf_op jit(solution)/shard_map/psum | solution.py:152
  904.9 1.6 convert_element_type.49
  906.5 1.6 convert_element_type.50
  (302 shorter events, 238.1 us)
Async XLA Ops:
  7.2 7.1 copy-start.12
  7.2 289.2 %all-gather.6.cloned.1.call-start = ((), (), s32[]{:S(2)}) async-start(), calls=%async_computation.4 | async-start | bytes 68157440 | tf_op jit(solution)/shard_map/all_gather | solution.py:11
  8.9 0.7 copy-start.4
  11.2 4.8 copy-start.7
  11.2 7.9 copy-start.10
  14.2 1.8 copy-start.1
  14.2 4.9 copy-start.2
  16.0 559.0 %all-gather.8.cloned.1.call-start = ((), (), s32[]{:S(2)}) async-start(), calls=%async_computation.5 | async-start | bytes 68157440 | tf_op jit(solution)/shard_map/all_gather | solution.py:11
  19.0 1.8 copy-start
  19.0 194.8 %copy-start.3 = (f32[4,8,512]{2,1,0:T(8,128)S(1)}, f32[4,8,512]{2,1,0:T(8,128)}, u32[]{:S(2)}) copy-start(f32[4,8,512]{2,1,0:T(8,128)} %param.15) | copy-start | bytes 196612
  19.1 194.8 %copy-start.14 = (f32[4,8]{1,0:T(4,128)S(1)}, f32[4,8]{1,0:T(4,128)}, u32[]{:S(2)}) copy-start(f32[4,8]{1,0:T(4,128)} %param.16) | copy-start | bytes 388
  20.8 884.1 %reduce-scatter.3.cloned.1.call-start = ((), (), s32[]{:S(2)}) async-start(), calls=%async_computation.2 | async-start | bytes 786432 | tf_op jit(solution)/shard_map/reduce_scatter | solution.py:147
  341.6 139.1 %copy-start.11 = (f32[512,4,8]{0,2,1:T(8,128)S(1)}, f32[512,4,8]{0,2,1:T(8,128)}, u32[]{:S(2)}) copy-start(f32[512,4,8]{0,2,1:T(8,128)} %copy-done.10) | copy-start | bytes 196612
  483.8 422.8 %reduce-scatter.5.cloned.1.call-start = ((), (), s32[]{:S(2)}) async-start(), calls=%async_computation.3 | async-start | bytes 786432 | tf_op jit(solution)/shard_map/reduce_scatter | solution.py:148
  575.0 135.5 %copy-start.8 = (f32[512,4,8]{0,2,1:T(8,128)S(1)}, f32[512,4,8]{0,2,1:T(8,128)}, u32[]{:S(2)}) copy-start(f32[512,4,8]{0,2,1:T(8,128)} %copy-done.7) | copy-start | bytes 196612
  710.4 3.1 copy-start.6
  710.4 3.1 copy-start.9
  719.2 4.8 copy-start.13
  719.5 7.0 copy-start.5
  719.5 7.0 copy-start.15
Sparse Core Ops, SparseCore 0:
  16.1 280.1 all-gather.5
  299.2 275.7 all-gather.7
  577.3 10.0 reduce-scatter.2
  713.6 10.1 reduce-scatter.4
where the time goes:
time: 924 us; the launch traced here: 915 us
  blocking collectives  368 us (40%)
  other arithmetic  197 us (21%)
  local copies, waits for them, and re-layouts  148 us (16%)
  waiting for transfers between devices  114 us (12%)
  matrix products  71.2 us (8%)
  between operations  14.1 us (2%)
    all_gather x1, blocking collectives, prefix(): pieces = jax.tree.map(lambda part: lax.all_gather(part, axis), value)  191 us
    select_n x126, other arithmetic, lap(): jnp.where(position < mine, new, old)  186 us
    psum x1, blocking collectives, body(): grad_alog, grad_bias = lax.psum((alog_term, bias_term), 'ctx')  177 us
    all_gather x2, waiting for transfers between devices, prefix(): pieces = jax.tree.map(lambda part: lax.all_gather(part, axis), value)  114 us
    mul x126, local copies, waits for them, and re-layouts, combine(): later[0][:, :, None, None] * earlier[1] + later[1]  85.8 us
    rev x2, local copies, waits for them, and re-layouts, prefix(): pieces = jax.tree.map(lambda part: part[::-1], pieces)  46.9 us
    dot_general x4, matrix products, within_block(): jnp.einsum('lhp,mhp->hlm', grad_g, inputs_g, preferred_element_type=jnp.f...  24.3 us
    dot_general x4, matrix products, within_block(): jnp.einsum('hlm,lhp->mhp', mixing, grad_g, preferred_element_type=jnp.flo...  19.9 us
  transfers between devices with their start and end apart: 4, of which 2 were waited for; matrix products, arithmetic and copies ran while one was open for 44% of the time, Pallas kernels for 0%

commit v1 on v0

v1 whole, which is shorter than its diff:
```python
import functools

import jax
import jax.numpy as jnp
from jax import lax
from jax.experimental import pallas as pl
from jax.experimental.pallas import tpu as pltpu
from jax.sharding import PartitionSpec as P

HIGHEST = lax.Precision.HIGHEST
F32 = jnp.float32
BF16 = jnp.bfloat16
MESH = pl.DeviceIdType.MESH

TOK = 512
GROUPS = 4
HEADS = 8
DIM = 64
CHUNK = 64
CHUNKS = TOK // CHUNK
PAIRS = CHUNKS // 2
ROWS = CHUNK * GROUPS
WIDE = HEADS * DIM
GH = GROUPS * HEADS
TILES = 64


def iota(shape, axis):
    return lax.broadcasted_iota(jnp.int32, shape, axis)


def ones(condition, kind=F32):
    return jnp.where(condition, 1.0, 0.0).astype(kind)


def dot(a, b, contract=((1,), (0,)), precision=None):
    return lax.dot_general(a, b, (contract, ((), ())), preferred_element_type=F32, precision=precision)


NT = ((1,), (1,))
TN = ((0,), (0,))


def kernel(
    n, x_ref, g_ref, dt_ref, bias_ref, alog_ref, bt_ref, ct_ref,
    gin_ref, graw_ref, galog_ref, gbias_ref, gb_ref, gc_ref,
    st_ref, sx_ref, xt_ref, gt_ref, bzt_ref, czt_ref, bz_ref, cz_ref, e_ref, f_ref, mul_ref,
    s_ref, g2_ref, sp_ref, gp_ref, z_ref, q_ref, gbacc_ref, gcacc_ref, th_ref,
    r2_ref, r2t_ref, gmask_ref, low_ref, wmask_ref,
    decsrc_ref, decall_ref, decx_ref, snd1_ref, rcv1_ref, snd2_ref, rcv2_ref,
    tsnd_ref, trcv_ref, tail_ref, tailall_ref,
    ss0, rs0, ss1, rs1, ss2, rs2, ss3, rs3, st4, rt4,
):
    m = TILES // n
    me = lax.axis_index("ctx")
    core = lax.axis_index("tp")
    other = 1 - core

    barrier = pltpu.get_barrier_semaphore()

    def greet(i, _):
        pl.semaphore_signal(barrier, inc=1, device_id=(lax.rem(me + i, n), core), device_id_type=MESH)
        return 0

    lax.fori_loop(1, n, greet, 0)
    pl.semaphore_signal(barrier, inc=1, device_id=(me, other), device_id_type=MESH)

    def to_peer(src, dst, ssem, rsem, i):
        peer = lax.rem(me + i, n)
        return pltpu.make_async_remote_copy(
            src_ref=src(peer), dst_ref=dst.at[me], send_sem=ssem.at[i], recv_sem=rsem.at[i],
            device_id=(peer, core), device_id_type=MESH,
        )

    def each_peer(action):
        def lap(i, _):
            action(i)
            return 0

        lax.fori_loop(1, n, lap, 0)

    diag = iota((HEADS, HEADS), 0) == iota((HEADS, HEADS), 1)

    def column(ref):
        return jnp.concatenate(
            [jnp.sum(jnp.where(diag, ref[g : g + 1, :], 0.0), axis=1, keepdims=True) for g in range(GROUPS)], axis=0
        )

    rates = jnp.exp(column(alog_ref))
    u = dt_ref[...] + column(bias_ref)
    step = jnp.maximum(u, 0.0) + jnp.log1p(jnp.exp(-jnp.abs(u)))
    ld = -step * rates
    sq0, sq1 = iota((128, 128), 0), iota((128, 128), 1)
    same = sq0 // CHUNK == sq1 // CHUNK
    tri = ones(same & (sq0 <= sq1))
    block = ones(same)

    def along_tokens(value, table):
        return jnp.concatenate(
            [dot(value[:, 128 * j : 128 * j + 128], table, precision=HIGHEST) for j in range(TOK // 128)], axis=1
        )

    cum = along_tokens(ld, tri)
    half = along_tokens(ld, block) * 0.5
    sg = jnp.exp(cum - half)
    sx = step * jnp.exp(half - cum)
    sg_hi = sg.astype(BF16).astype(F32)
    sx_hi = sx.astype(BF16).astype(F32)
    stack = jnp.concatenate([sg_hi, sg - sg_hi, sx_hi, sx - sx_hi], axis=0)
    for j in range(TOK // 128):
        st_ref[128 * j : 128 * j + 128, :] = stack[:, 128 * j : 128 * j + 128].T.astype(BF16)

    total = jnp.sum(ld, axis=1, keepdims=True)
    row = jnp.sum(jnp.where(iota((GH, 128), 0) == iota((GH, 128), 1), total, 0.0), axis=0, keepdims=True)
    decsrc_ref[...] = jnp.broadcast_to(row, (8, 128))
    decall_ref[me] = decsrc_ref[...]
    pl.semaphore_wait(barrier, n)
    dec_copy = functools.partial(to_peer, lambda peer: decsrc_ref, decall_ref, ss0, rs0)
    each_peer(lambda i: dec_copy(i).start())

    first = ones(iota((TOK, CHUNKS * GROUPS), 0) == (iota((TOK, CHUNKS * GROUPS), 1) // GROUPS) * CHUNK)
    half8 = dot(half, first, precision=HIGHEST)
    half8 = jnp.where(iota((GH, 32), 0) // HEADS == iota((GH, 32), 1) % GROUPS, half8, 0.0)
    by_head = ones(iota((GH, WIDE), 0) % HEADS == iota((GH, WIDE), 1) // DIM)
    mul_ref[...] = jnp.exp(dot(half8, by_head, TN, HIGHEST))

    r2_ref[...] = ones(iota((128, 512), 0) == iota((128, 512), 1) // GROUPS, BF16)
    r2t_ref[...] = ones(iota((512, 128), 1) == iota((512, 128), 0) // GROUPS, BF16)
    gmask_ref[...] = ones(iota((256, 512), 0) // DIM == iota((256, 512), 1) % GROUPS)
    low = iota((ROWS, ROWS), 0) // GROUPS >= iota((ROWS, ROWS), 1) // GROUPS
    low_ref[...] = ones(low)
    wmask_ref[...] = ones(low & (iota((ROWS, ROWS), 0) % GROUPS == iota((ROWS, ROWS), 1) % GROUPS))
    lane128 = iota((128, WIDE), 0)
    col128 = iota((128, WIDE), 1) // DIM
    eg = ones((lane128 // 64 == 0) & (lane128 % HEADS == col128), BF16)
    ex = ones((lane128 // 64 == 1) & (lane128 % HEADS == col128), BF16)
    mask4 = ones((iota((512, 128), 1) // HEADS) % GROUPS == iota((512, 128), 0) % GROUPS)
    rmask = ones(iota((512, 256), 0) % GROUPS == iota((512, 256), 1) // DIM)

    def pair_rows(i, k):
        return pl.ds(pl.multiple_of(i * 512 + k * 256, 256), 256)

    def pair_lanes(i):
        return pl.ds(pl.multiple_of(i * 128, 128), 128)

    def scale_pair(i, _):
        spread = dot(r2t_ref[...], st_ref[pair_lanes(i), :]) * mask4
        spread = spread.astype(BF16)
        b_pair, c_pair = bt_ref[:, pair_lanes(i)], ct_ref[:, pair_lanes(i)]
        bzt = (dot(b_pair, r2_ref[...]) * gmask_ref[...]).astype(BF16)
        czt = (dot(c_pair, r2_ref[...]) * gmask_ref[...]).astype(BF16)
        bz_ref[pl.ds(pl.multiple_of(i * 512, 512), 512), :] = (dot(r2t_ref[...], b_pair, NT) * rmask).astype(BF16)
        cz_ref[pl.ds(pl.multiple_of(i * 512, 512), 512), :] = (dot(r2t_ref[...], c_pair, NT) * rmask).astype(BF16)
        for k in range(2):
            part = spread[256 * k : 256 * k + 256]
            rows = pair_rows(i, k)
            tokens = pl.ds(i * 128 + k * 64, 64)
            scale = dot(part, ex)
            sx_ref[rows, :] = scale
            xt = (x_ref[tokens].reshape(ROWS, WIDE).astype(F32) * scale).astype(BF16)
            xt_ref[rows, :] = xt
            gt = (g_ref[tokens].reshape(ROWS, WIDE).astype(F32) * dot(part, eg)).astype(BF16)
            gt_ref[rows, :] = gt
            bz_k, cz_k = bzt[:, 256 * k : 256 * k + 256], czt[:, 256 * k : 256 * k + 256]
            bzt_ref[i * 2 + k] = bz_k
            czt_ref[i * 2 + k] = cz_k
            e_ref[i * 2 + k] = dot(bz_k, xt)
            f_ref[i * 2 + k] = dot(cz_k, gt)
        return 0

    lax.fori_loop(0, PAIRS, scale_pair, 0)

    def advance(state_ref, add_ref, c, low_out):
        for g in range(GROUPS):
            rows = slice(DIM * g, DIM * g + DIM)
            factor = mul_ref[pl.ds(c * GROUPS + g, 1), :]
            scaled = factor * state_ref[rows, :]
            if low_out is not None:
                low_out[c, rows, :] = scaled.astype(BF16)
            state_ref[rows, :] = factor * (scaled + add_ref[c, rows, :])

    def scan_chunks(s_low, g_low):
        def lap(c, _):
            advance(s_ref, e_ref, c, s_low)
            advance(g2_ref, f_ref, CHUNKS - 1 - c, g_low)
            return 0

        lax.fori_loop(0, CHUNKS, lap, 0)

    s_ref[...] = jnp.zeros_like(s_ref)
    g2_ref[...] = jnp.zeros_like(g2_ref)
    scan_chunks(None, None)
    for t in range(TILES):
        rows, lanes = slice(16 * (t // 4), 16 * (t // 4) + 16), slice(128 * (t % 4), 128 * (t % 4) + 128)
        snd1_ref[t // m, t % m, 0] = s_ref[rows, lanes].astype(BF16)
        snd1_ref[t // m, t % m, 1] = g2_ref[rows, lanes].astype(BF16)
    rcv1_ref[me] = snd1_ref[me]
    copy1 = functools.partial(to_peer, lambda peer: snd1_ref.at[peer], rcv1_ref, ss1, rs1)
    each_peer(lambda i: copy1(i).start())

    es_row = iota((WIDE, 128), 0) // DIM
    es_lane = iota((WIDE, 128), 1)

    def fold(kind):
        return ones((es_lane // GH == kind) & (es_lane % HEADS == es_row), BF16)

    def gather_rows(d, k):
        r = ones(iota((CHUNK, ROWS), 0) == iota((CHUNK, ROWS), 1) // GROUPS)
        return dot(r, d * mask4[:ROWS], precision=HIGHEST)

    def exact_fold(value, kind):
        hi = value.astype(BF16)
        lo = (value - hi.astype(F32)).astype(BF16)
        return dot(hi, fold(kind)) + dot(lo, fold(kind))

    def local_pair(i, _):
        gbs, gcs = [], []
        for k in range(2):
            c = i * 2 + k
            rows = pair_rows(i, k)
            xt, gt = xt_ref[rows, :], gt_ref[rows, :]
            bzt, czt = bzt_ref[c], czt_ref[c]
            mix = (dot(cz_ref[rows, :], bzt) * low_ref[...]).astype(BF16)
            mix_t = (dot(bz_ref[rows, :], czt) * low_ref[...].T).astype(BF16)
            y = dot(mix, xt)
            z = dot(mix_t, gt)
            z_ref[rows, :] = z
            d = exact_fold(gt.astype(F32) * y, 0) + exact_fold(xt.astype(F32) * z, 1)
            q_ref[pl.ds(i * 128 + k * 64, 64), :] = gather_rows(d, k)
            w = jnp.where(wmask_ref[...] > 0.5, dot(gt, xt, NT), 0.0).astype(BF16)
            gbs.append(dot(czt, w).astype(BF16))
            gcs.append(dot(bzt, w, NT).astype(BF16))
        gbacc_ref[:, pair_lanes(i)] = dot(jnp.concatenate(gbs, axis=1), r2t_ref[...])
        gcacc_ref[:, pair_lanes(i)] = dot(jnp.concatenate(gcs, axis=1), r2t_ref[...])
        return 0

    lax.fori_loop(0, PAIRS // 2, local_pair, 0)

    each_peer(lambda i: dec_copy(i).wait())
    each_peer(lambda i: copy1(i).wait())
    table = decall_ref[:, 0, :]
    for t in range(m):
        tile = me * m + t
        head = (tile // 16) * HEADS + (tile % 4) * 2 + sq1 // DIM
        decx_ref[t] = jnp.exp(dot(table, ones(sq0 == head), precision=HIGHEST))

    def lap(k, carry):
        back = n - 1 - k
        out = []
        for t in range(m):
            s, g = carry[2 * t], carry[2 * t + 1]
            snd2_ref[k, t, 0] = s.astype(BF16)
            snd2_ref[back, t, 1] = g.astype(BF16)
            s = decx_ref[t, pl.ds(k, 1), :] * s + rcv1_ref[k, t, 0].astype(F32)
            g = decx_ref[t, pl.ds(back, 1), :] * g + rcv1_ref[back, t, 1].astype(F32)
            out += [s, g]
        return tuple(out)

    lax.fori_loop(0, n, lap, tuple(jnp.zeros((16, 128), F32) for _ in range(2 * m)))
    rcv2_ref[me] = snd2_ref[me]
    copy2 = functools.partial(to_peer, lambda peer: snd2_ref.at[peer], rcv2_ref, ss2, rs2)
    each_peer(lambda i: copy2(i).start())

    lax.fori_loop(PAIRS // 2, PAIRS, local_pair, 0)

    each_peer(lambda i: copy2(i).wait())
    for t in range(TILES):
        rows, lanes = slice(16 * (t // 4), 16 * (t // 4) + 16), slice(128 * (t % 4), 128 * (t % 4) + 128)
        s_ref[rows, lanes] = rcv2_ref[t // m, t % m, 0].astype(F32)
        g2_ref[rows, lanes] = rcv2_ref[t // m, t % m, 1].astype(F32)
    scan_chunks(sp_ref, gp_ref)

    def cross_pair(i, _):
        gbs, gcs = [], []
        for k in range(2):
            c = i * 2 + k
            rows = pair_rows(i, k)
            tokens = pl.ds(i * 128 + k * 64, 64)
            xt, gt = xt_ref[rows, :], gt_ref[rows, :]
            sp, gp = sp_ref[c], gp_ref[c]
            through = sp.astype(F32) * gp.astype(F32)
            for g in range(GROUPS):
                part = jnp.sum(through[DIM * g : DIM * g + DIM], axis=0, keepdims=True)
                th_ref[pl.ds(c * GROUPS + g, 1), :] = part
            out = dot(cz_ref[rows, :], sp)
            back = dot(bz_ref[rows, :], gp)
            d = dot((gt.astype(F32) * out).astype(BF16), fold(0)) + dot((xt.astype(F32) * back).astype(BF16), fold(2))
            q_ref[tokens, :] = q_ref[tokens, :] + gather_rows(d, k)
            gin = (sx_ref[rows, :] * (z_ref[rows, :] + back)).astype(BF16)
            gin_ref[tokens] = gin.reshape(CHUNK, GROUPS, WIDE)
            gbs.append((dot(gp, xt, NT) * gmask_ref[:, :256]).astype(BF16))
            gcs.append((dot(sp, gt, NT) * gmask_ref[:, :256]).astype(BF16))
        gbacc_ref[:, pair_lanes(i)] = gbacc_ref[:, pair_lanes(i)] + dot(jnp.concatenate(gbs, axis=1), r2t_ref[...])
        gcacc_ref[:, pair_lanes(i)] = gcacc_ref[:, pair_lanes(i)] + dot(jnp.concatenate(gcs, axis=1), r2t_ref[...])
        return 0

    lax.fori_loop(0, PAIRS, cross_pair, 0)

    theirs = pl.ds(pl.multiple_of(other * 128, 128), 128)
    mine = pl.ds(pl.multiple_of(core * 128, 128), 128)
    tsnd_ref[0] = gbacc_ref[theirs, :].astype(BF16)
    tsnd_ref[1] = gcacc_ref[theirs, :].astype(BF16)
    swap = pltpu.make_async_remote_copy(
        src_ref=tsnd_ref, dst_ref=trcv_ref, send_sem=st4, recv_sem=rt4, device_id=(me, other), device_id_type=MESH
    )
    swap.start()

    qt = jnp.concatenate([q_ref[128 * j : 128 * j + 128, :].T for j in range(TOK // 128)], axis=1)
    inner, local, outer = qt[0:GH], qt[GH : 2 * GH], qt[2 * GH : 3 * GH]
    th = dot(th_ref[...], ones(iota((WIDE, GH), 0) // DIM == iota((WIDE, GH), 1) % HEADS), precision=HIGHEST)
    th = jnp.where(iota((32, GH), 0) % GROUPS == iota((32, GH), 1) // HEADS, th, 0.0)
    spread_th = ones(iota((32, TOK), 0) // GROUPS == iota((32, TOK), 1) // CHUNK)
    suffix = ones(same & (sq0 >= sq1))
    before = ones(same & (sq0 < sq1))
    log_grad = (
        along_tokens(inner - local, suffix) + along_tokens(outer, before) + dot(th, spread_th, TN, HIGHEST)
    )
    sig = 1.0 / (1.0 + jnp.exp(-u))
    graw = ((local + outer) / step - rates * log_grad) * sig
    graw_ref[...] = graw
    alog_col = jnp.sum(log_grad * ld, axis=1, keepdims=True)
    bias_col = jnp.sum(graw, axis=1, keepdims=True)
    pick = iota((GH, 128), 0) == iota((GH, 128), 1)
    alog_row = jnp.sum(jnp.where(pick, alog_col, 0.0), axis=0, keepdims=True)
    bias_row = jnp.sum(jnp.where(pick, bias_col, 0.0), axis=0, keepdims=True)
    tail_ref[...] = jnp.where(iota((8, 128), 0) < 4, alog_row, bias_row)
    tailall_ref[me] = tail_ref[...]
    tail_copy = functools.partial(to_peer, lambda peer: tail_ref, tailall_ref, ss3, rs3)
    each_peer(lambda i: tail_copy(i).start())

    swap.wait()
    gb_ref[...] = (gbacc_ref[mine, :] + trcv_ref[0].astype(F32)).astype(BF16)
    gc_ref[...] = (gcacc_ref[mine, :] + trcv_ref[1].astype(F32)).astype(BF16)

    each_peer(lambda i: tail_copy(i).wait())
    sums = jnp.sum(tailall_ref[...], axis=0)
    sums = jnp.where(iota((8, 128), 1) // HEADS == iota((8, 128), 0) % GROUPS, sums, 0.0)
    ends = dot(sums, ones(iota((128, HEADS), 0) % HEADS == iota((128, HEADS), 1)), precision=HIGHEST)
    galog_ref[...] = ends[0:4]
    gbias_ref[...] = ends[4:8]


def scratch(n):
    m = TILES // n
    dma = pltpu.SemaphoreType.DMA
    vm = pltpu.VMEM
    return [
        vm((TOK, 128), BF16), vm((2048, WIDE), F32), vm((2048, WIDE), BF16), vm((2048, WIDE), BF16),
        vm((CHUNKS, 256, 256), BF16), vm((CHUNKS, 256, 256), BF16), vm((2048, 256), BF16), vm((2048, 256), BF16),
        vm((CHUNKS, 256, WIDE), F32), vm((CHUNKS, 256, WIDE), F32), vm((32, WIDE), F32),
        vm((256, WIDE), F32), vm((256, WIDE), F32), vm((CHUNKS, 256, WIDE), BF16), vm((CHUNKS, 256, WIDE), BF16),
        vm((2048, WIDE), F32), vm((TOK, 128), F32), vm((256, TOK), F32), vm((256, TOK), F32), vm((32, WIDE), F32),
        vm((128, 512), BF16), vm((512, 128), BF16), vm((256, 512), F32), vm((ROWS, ROWS), F32), vm((ROWS, ROWS), F32),
        vm((8, 128), F32), vm((n, 8, 128), F32), vm((m, n, 128), F32),
        vm((n, m, 2, 16, 128), BF16), vm((n, m, 2, 16, 128), BF16), vm((n, m, 2, 16, 128), BF16), vm((n, m, 2, 16, 128), BF16),
        vm((2, 128, TOK), BF16), vm((2, 128, TOK), BF16), vm((8, 128), F32), vm((n, 8, 128), F32),
        dma((n,)), dma((n,)), dma((n,)), dma((n,)), dma((n,)), dma((n,)), dma((n,)), dma((n,)), dma, dma,
    ]


def solution(mesh):
    n = mesh.shape["ctx"]

    def body(inputs, grad_out, dt_raw, dt_bias, a_log, b_proj, c_proj):
        bt = jnp.transpose(b_proj, (1, 2, 0)).reshape(GROUPS * DIM, TOK)
        ct = jnp.transpose(c_proj, (1, 2, 0)).reshape(GROUPS * DIM, TOK)
        vmem = pl.BlockSpec(memory_space=pltpu.VMEM)
        gin, graw, galog, gbias, gb, gc = pl.pallas_call(
            functools.partial(kernel, n),
            out_shape=[
                jax.ShapeDtypeStruct((TOK, GROUPS, WIDE), BF16),
                jax.ShapeDtypeStruct((GH, TOK), F32),
                jax.ShapeDtypeStruct((GROUPS, HEADS), F32),
                jax.ShapeDtypeStruct((GROUPS, HEADS), F32),
                jax.ShapeDtypeStruct((128, TOK), BF16),
                jax.ShapeDtypeStruct((128, TOK), BF16),
            ],
            in_specs=[vmem] * 7,
            out_specs=[vmem] * 6,
            scratch_shapes=scratch(n),
            compiler_params=pltpu.CompilerParams(
                collective_id=0, has_side_effects=True, vmem_limit_bytes=58 * 2**20
            ),
        )(inputs, grad_out, dt_raw.reshape(GH, TOK), dt_bias, a_log, bt, ct)
        graw = graw.reshape(GROUPS, HEADS, TOK)
        gb = jnp.transpose(gb.reshape(2, DIM, TOK), (2, 0, 1))
        gc = jnp.transpose(gc.reshape(2, DIM, TOK), (2, 0, 1))
        return gin, graw, galog, gbias, gb, gc

    in_specs = (
        P("ctx", None, "tp"),
        P("ctx", None, "tp"),
        P(None, "tp", "ctx"),
        P(None, "tp"),
        P(None, "tp"),
        P("ctx", None, None),
        P("ctx", None, None),
    )
    out_specs = (
        P("ctx", None, "tp"),
        P(None, "tp", "ctx"),
        P(None, "tp"),
        P(None, "tp"),
        P("ctx", "tp", None),
        P("ctx", "tp", None),
    )
    return jax.shard_map(body, mesh=mesh, in_specs=in_specs, out_specs=out_specs, check_vma=False)
```

time: 924 us -> 69.6 us (0.08)
  blocking collectives: 368 us -> 0 us
  other arithmetic: 197 us -> 0 us
  local copies, waits for them, and re-layouts: 148 us -> 6.79 us
  waiting for transfers between devices: 114 us -> 0 us
  matrix products: 71.2 us -> 0 us
  Pallas kernels: 0 us -> 61.9 us
  between operations: 14.1 us -> 0.69 us
    all_gather x1 -> x0, blocking collectives: 191 us -> none  [prefix(): pieces = jax.tree.map(lambda part: lax.all_gather(part, axis), value)]
    select_n x127 -> x0, other arithmetic: 187 us -> none  [the longest x126 186 us: lap(): jnp.where(position < mine, new, old)]
    psum x1 -> x0, blocking collectives: 177 us -> none  [body(): grad_alog, grad_bias = lax.psum((alog_term, bias_term), 'ctx')]
    all_gather x2 -> x0, waiting for transfers between devices: 114 us -> none  [prefix(): pieces = jax.tree.map(lambda part: lax.all_gather(part, axis), value)]
    mul x130 -> x0, local copies, waits for them, and re-layouts: 88.7 us -> none  [the longest x126 85.8 us: combine(): later[0][:, :, None, None] * earlier[1] + later[1]]
    dot_general x28 -> x0, matrix products: 71.2 us -> none  [the longest x4 24.3 us: within_block(): jnp.einsum('lhp,mhp->hlm', grad_g, inputs_g, preferred_element_type=jnp.f...]
    pallas_call x0 -> x1, Pallas kernels: none -> 61.9 us  [body(): pl.pallas_call(functools.partial(kernel, n), out_shape=[jax.ShapeDtypeStr...]
    rev x2 -> x0, local copies, waits for them, and re-layouts: 46.9 us -> none  [prefix(): pieces = jax.tree.map(lambda part: part[::-1], pieces)]
  transfers between devices with their start and end apart: 4 -> 0, of which waited for: 2 -> 0; matrix products, arithmetic and copies ran while one was open for 44% -> 0% of each run, Pallas kernels for 0% -> 0%
where the time goes in v1:
time: 69.6 us; the launch traced here: 69.4 us
  Pallas kernels  61.9 us (89%)
  local copies, waits for them, and re-layouts  6.79 us (10%)
    pallas_call x1, Pallas kernels, body(): pl.pallas_call(functools.partial(kernel, n), out_shape=[jax.ShapeDtypeStr...  61.9 us
    unnamed x16, local copies, waits for them, and re-layouts  6.79 us

profile of v1, /device:TPU:0, one launch (start us, length us, event | category | flops | bytes accessed | tf_op | source)
XLA Modules:
  0.0 69.4 jit_solution(12936853065691845496)
XLA Ops:
  0.6 61.9 %shard_map.118 = (bf16[512,4,512]{2,1,0:T(4,128)(2,1)}, f32[32,512]{1,0:T(8,128)}, f32[4,8]{1,0:T(4,128)}, f32[4,8]{1,0:T(4,128)}, bf16[128,512]{1,0:T(8,128)(2,1)}, /*index=5*/bf16[128,512]{1,0:T(8,128)(2,1)}) custom-call(bf16[512,4,512]{2,1,0:T(4,128)(2,1)} %x_ref.1, bf16[512,4,512]{2,1,0:T(4,128)(2,1)} %g_ref.1, f32[32,512]{1,0:T(8,128)} %bitcast.18, ...), custom_call_target="tpu_custom_call" | custom-call | tf_op jit(solution)/shard_map/pallas_call | solution.py:368
  62.6 0.0 copy-start.2
  62.6 0.0 copy-start.4
  62.6 0.0 copy-start.3
  62.6 0.0 copy-start.1
  62.6 0.0 copy-start
  62.6 3.7 %copy.19 = bf16[512,4,512]{2,1,0:T(4,128)(2,1)} copy(bf16[512,4,512]{2,1,0:T(4,128)(2,1)} %get-tuple-element.24) | data formatting | bytes 4194304
  66.3 0.0 copy-done.2
  66.3 0.6 copy.20
  66.9 0.0 copy-done.4
  66.9 0.6 copy.21
  67.5 0.0 copy-done.3
  67.5 0.6 copy.22
  68.1 0.0 copy-done.1
  68.1 0.7 copy.23
  68.8 0.0 copy-done
  68.8 0.7 copy.24
Async XLA Ops:
  62.6 3.7 %copy-start.2 = (f32[32,512]{1,0:T(8,128)S(1)}, f32[32,512]{1,0:T(8,128)}, u32[]{:S(2)}) copy-start(f32[32,512]{1,0:T(8,128)} %get-tuple-element.13) | copy-start | bytes 196612
  62.6 4.3 %copy-start.4 = (f32[4,8]{1,0:T(4,128)S(1)}, f32[4,8]{1,0:T(4,128)}, u32[]{:S(2)}) copy-start(f32[4,8]{1,0:T(4,128)} %get-tuple-element.26) | copy-start | bytes 388
  62.6 4.9 %copy-start.3 = (f32[4,8]{1,0:T(4,128)S(1)}, f32[4,8]{1,0:T(4,128)}, u32[]{:S(2)}) copy-start(f32[4,8]{1,0:T(4,128)} %get-tuple-element.27) | copy-start | bytes 388
  62.6 5.5 %copy-start.1 = (bf16[128,512]{1,0:T(8,128)(2,1)S(1)}, bf16[128,512]{1,0:T(8,128)(2,1)}, u32[]{:S(2)}) copy-start(bf16[128,512]{1,0:T(8,128)(2,1)} %get-tuple-element.16) | copy-start | bytes 393220
  62.6 6.1 %copy-start = (bf16[128,512]{1,0:T(8,128)(2,1)S(1)}, bf16[128,512]{1,0:T(8,128)(2,1)}, u32[]{:S(2)}) copy-start(bf16[128,512]{1,0:T(8,128)(2,1)} %get-tuple-element.17) | copy-start | bytes 393220

commit v2 on v1

v2 whole, which is shorter than its diff:
```python
import functools

import jax
import jax.numpy as jnp
from jax import lax
from jax.experimental import pallas as pl
from jax.experimental.pallas import tpu as pltpu
from jax.sharding import PartitionSpec as P

HIGHEST = lax.Precision.HIGHEST
F32 = jnp.float32
BF16 = jnp.bfloat16
MESH = pl.DeviceIdType.MESH

TOK = 512
GROUPS = 4
HEADS = 8
DIM = 64
CHUNK = 64
CHUNKS = TOK // CHUNK
PAIRS = CHUNKS // 2
ROWS = CHUNK * GROUPS
WIDE = HEADS * DIM
GH = GROUPS * HEADS
TILES = 64


def iota(shape, axis):
    return lax.broadcasted_iota(jnp.int32, shape, axis)


def over(value, size):
    return lax.shift_right_logical(value, size.bit_length() - 1)


def within(value, size):
    return value & (size - 1)


def ones(condition, kind=F32):
    return jnp.where(condition, 1.0, 0.0).astype(kind)


def dot(a, b, contract=((1,), (0,)), precision=None):
    return lax.dot_general(a, b, (contract, ((), ())), preferred_element_type=F32, precision=precision)


NT = ((1,), (1,))
TN = ((0,), (0,))


def kernel(
    n, x_hbm, g_hbm, dt_ref, bias_ref, alog_ref, bt_ref, ct_ref,
    gin_hbm, graw_ref, galog_ref, gbias_ref, gb_ref, gc_ref,
    x_ref, g_ref, gin_ref, st_ref, spread_ref, sx_ref, xt_ref, gt_ref, bzt_ref, czt_ref, bz_ref, cz_ref,
    e_ref, f_ref, mul_ref, s_ref, g2_ref, sp_ref, gp_ref, z_ref, lg_ref, al_ref, gbacc_ref, gcacc_ref, th_ref,
    step_ref, ld_ref, r2_ref, r2t_ref, low_ref, lowt_ref, wmask_ref,
    decsrc_ref, decall_ref, decx_ref, esnd_ref, ercv_ref, fsnd_ref, frcv_ref, ssnd_ref, srcv_ref, gsnd_ref, grcv_ref,
    tsnd_ref, trcv_ref, tail_ref, tailall_ref,
    ss0, rs0, sse, rse, ssf, rsf, sss, rss, ssg, rsg, ss3, rs3, st4, rt4, ld4, out4,
):
    m = TILES // n
    me = lax.axis_index("ctx")
    core = lax.axis_index("tp")
    other = 1 - core

    barrier = pltpu.get_barrier_semaphore()

    def greet(i, _):
        pl.semaphore_signal(barrier, inc=1, device_id=(lax.rem(me + i, n), core), device_id_type=MESH)
        return 0

    load_x = pltpu.make_async_copy(x_hbm, x_ref, ld4.at[0])
    load_g = pltpu.make_async_copy(g_hbm, g_ref, ld4.at[1])
    load_x.start()
    load_g.start()
    lax.fori_loop(1, n, greet, 0)
    pl.semaphore_signal(barrier, inc=1, device_id=(me, other), device_id_type=MESH)

    def to_peer(src, dst, ssem, rsem, i):
        peer = lax.rem(me + i, n)
        return pltpu.make_async_remote_copy(
            src_ref=src(peer), dst_ref=dst.at[me], send_sem=ssem, recv_sem=rsem,
            device_id=(peer, core), device_id_type=MESH,
        )

    def settle(dst, ssem, rsem):
        every = dst.at[pl.ds(0, n - 1)]
        pltpu.make_async_remote_copy(
            src_ref=every, dst_ref=every, send_sem=ssem, recv_sem=rsem,
            device_id=(me, other), device_id_type=MESH,
        ).wait()

    def each_peer(action):
        def lap(i, _):
            action(i)
            return 0

        lax.fori_loop(1, n, lap, 0)

    diag = iota((HEADS, HEADS), 0) == iota((HEADS, HEADS), 1)

    def column(ref):
        return jnp.concatenate(
            [jnp.sum(jnp.where(diag, ref[g : g + 1, :], 0.0), axis=1, keepdims=True) for g in range(GROUPS)], axis=0
        )

    rates = jnp.exp(column(alog_ref))
    u = dt_ref[...] + column(bias_ref)
    step = jnp.maximum(u, 0.0) + jnp.log1p(jnp.exp(-jnp.abs(u)))
    ld = -step * rates
    step_ref[...] = step
    ld_ref[...] = ld
    sq0, sq1 = iota((128, 128), 0), iota((128, 128), 1)
    same = over(sq0, CHUNK) == over(sq1, CHUNK)
    tri = ones(same & (sq0 <= sq1))
    block = ones(same)

    def along_tokens(value, table):
        return jnp.concatenate(
            [dot(value[:, 128 * j : 128 * j + 128], table, precision=HIGHEST) for j in range(TOK // 128)], axis=1
        )

    cum = along_tokens(ld, tri)
    half = along_tokens(ld, block) * 0.5
    sg = jnp.exp(cum - half)
    sx = step * jnp.exp(half - cum)
    sg_hi = sg.astype(BF16).astype(F32)
    sx_hi = sx.astype(BF16).astype(F32)
    stack = jnp.concatenate([sg_hi, sg - sg_hi, sx_hi, sx - sx_hi], axis=0)
    for j in range(TOK // 128):
        st_ref[128 * j : 128 * j + 128, :] = stack[:, 128 * j : 128 * j + 128].T.astype(BF16)

    total = jnp.sum(ld, axis=1, keepdims=True)
    row = jnp.sum(jnp.where(iota((GH, 128), 0) == iota((GH, 128), 1), total, 0.0), axis=0, keepdims=True)
    decsrc_ref[...] = row
    decall_ref[me] = decsrc_ref[...]

    first = ones(iota((TOK, CHUNKS * GROUPS), 0) == over(iota((TOK, CHUNKS * GROUPS), 1), GROUPS) * CHUNK)
    half8 = dot(half, first, precision=HIGHEST)
    half8 = jnp.where(over(iota((GH, 32), 0), HEADS) == within(iota((GH, 32), 1), GROUPS), half8, 0.0)
    by_head = ones(within(iota((GH, WIDE), 0), HEADS) == over(iota((GH, WIDE), 1), DIM))
    mul_ref[...] = jnp.exp(dot(half8, by_head, TN, HIGHEST))

    r2_ref[...] = ones(iota((128, 512), 0) == over(iota((128, 512), 1), GROUPS), BF16)
    r2t_ref[...] = ones(iota((512, 128), 1) == over(iota((512, 128), 0), GROUPS), BF16)
    gmask = ones(over(iota((256, 256), 0), DIM) == within(iota((256, 256), 1), GROUPS))
    lane128 = iota((128, WIDE), 0)
    col128 = over(iota((128, WIDE), 1), DIM)
    eg = ones((over(lane128, 64) == 0) & (within(lane128, HEADS) == col128), BF16)
    ex = ones((over(lane128, 64) == 1) & (within(lane128, HEADS) == col128), BF16)
    mask4 = ones(within(over(iota((ROWS, 128), 1), HEADS), GROUPS) == within(iota((ROWS, 128), 0), GROUPS))

    def pair_rows(i, k):
        return pl.ds(pl.multiple_of(i * 512 + k * 256, 256), 256)

    def pair_lanes(i):
        return pl.ds(pl.multiple_of(i * 128, 128), 128)

    def tokens_of(i, k):
        return pl.ds(i * 128 + k * 64, 64)

    def advance(state_ref, add_ref, c, low_out):
        for g in range(GROUPS):
            rows = slice(DIM * g, DIM * g + DIM)
            factor = mul_ref[pl.ds(c * GROUPS + g, 1), :]
            scaled = factor * state_ref[rows, :]
            if low_out is not None:
                low_out[c, rows, :] = scaled.astype(BF16)
            state_ref[rows, :] = factor * (scaled + add_ref[c, rows, :])

    def to_slices(state_ref, out_ref):
        for t in range(TILES):
            rows, lanes = slice(16 * (t // 4), 16 * (t // 4) + 16), slice(128 * (t % 4), 128 * (t % 4) + 128)
            out_ref[t // m, t % m] = state_ref[rows, lanes].astype(BF16)

    def from_slices(in_ref, state_ref):
        for t in range(TILES):
            rows, lanes = slice(16 * (t // 4), 16 * (t // 4) + 16), slice(128 * (t % 4), 128 * (t % 4) + 128)
            state_ref[rows, lanes] = in_ref[t // m, t % m].astype(F32)

    s_ref[...] = jnp.zeros_like(s_ref)
    g2_ref[...] = jnp.zeros_like(g2_ref)
    load_x.wait()

    def x_pair(i, _):
        bzt = dot(bt_ref[:, pair_lanes(i)], r2_ref[...])
        for k in range(2):
            rows = pair_rows(i, k)
            c = i * 2 + k
            part = (dot(r2t_ref[256 * k : 256 * k + 256, :], st_ref[pair_lanes(i), :]) * mask4).astype(BF16)
            spread_ref[rows, :] = part
            scale = dot(part, ex)
            sx_ref[rows, :] = scale
            xt = (x_ref[tokens_of(i, k)].reshape(ROWS, WIDE).astype(F32) * scale).astype(BF16)
            xt_ref[rows, :] = xt
            bz_k = (bzt[:, 256 * k : 256 * k + 256] * gmask).astype(BF16)
            bzt_ref[c] = bz_k
            e_ref[c] = dot(bz_k, xt)
            advance(s_ref, e_ref, c, None)
        return 0

    lax.fori_loop(0, PAIRS, x_pair, 0)
    to_slices(s_ref, esnd_ref)
    ercv_ref[me] = esnd_ref[me]
    pl.semaphore_wait(barrier, n)
    dec_copy = functools.partial(to_peer, lambda peer: decsrc_ref, decall_ref, ss0, rs0)
    each_peer(lambda i: dec_copy(i).start())
    copy_e = functools.partial(to_peer, lambda peer: esnd_ref.at[peer], ercv_ref, sse, rse)
    each_peer(lambda i: copy_e(i).start())

    load_g.wait()

    def g_pair(lap, _):
        i = PAIRS - 1 - lap
        czt = dot(ct_ref[:, pair_lanes(i)], r2_ref[...])
        for k in (1, 0):
            rows = pair_rows(i, k)
            c = i * 2 + k
            gt = (g_ref[tokens_of(i, k)].reshape(ROWS, WIDE).astype(F32) * dot(spread_ref[rows, :], eg)).astype(BF16)
            gt_ref[rows, :] = gt
            cz_k = (czt[:, 256 * k : 256 * k + 256] * gmask).astype(BF16)
            czt_ref[c] = cz_k
            f_ref[c] = dot(cz_k, gt)
            advance(g2_ref, f_ref, c, None)
        return 0

    lax.fori_loop(0, PAIRS, g_pair, 0)
    to_slices(g2_ref, fsnd_ref)
    frcv_ref[me] = fsnd_ref[me]
    copy_f = functools.partial(to_peer, lambda peer: fsnd_ref.at[peer], frcv_ref, ssf, rsf)
    each_peer(lambda i: copy_f(i).start())

    low = over(iota((ROWS, ROWS), 0), GROUPS) >= over(iota((ROWS, ROWS), 1), GROUPS)
    low_ref[...] = ones(low)
    lowt_ref[...] = ones(over(iota((ROWS, ROWS), 0), GROUPS) <= over(iota((ROWS, ROWS), 1), GROUPS))
    wmask_ref[...] = ones(low & (within(iota((ROWS, ROWS), 0), GROUPS) == within(iota((ROWS, ROWS), 1), GROUPS)))
    rmask = ones(within(iota((ROWS, 256), 0), GROUPS) == over(iota((ROWS, 256), 1), DIM))
    es_row = over(iota((WIDE, 128), 0), DIM)
    es_lane = iota((WIDE, 128), 1)
    fold_in = ones((over(es_lane, GH) == 0) & (within(es_lane, HEADS) == es_row), BF16)
    fold_out = ones((over(es_lane, GH) == 1) & (within(es_lane, HEADS) == es_row), BF16) - fold_in
    tr, tu = over(iota((512, 128), 0), GROUPS), iota((512, 128), 1)
    suffix = ones((tr >= tu) & (over(tr, CHUNK) == over(tu, CHUNK)), BF16)
    before = ones((tr < tu) & (over(tr, CHUNK) == over(tu, CHUNK)), BF16)
    plain = r2t_ref[...]
    suffix_plain = jnp.concatenate([suffix, plain], axis=1)
    before_plain = jnp.concatenate([before, plain], axis=1)

    def split(value):
        hi = value.astype(BF16)
        return hi, (value - hi.astype(F32)).astype(BF16)

    def exact_fold(value, table):
        hi, lo = split(value)
        return dot(hi, table) + dot(lo, table)

    def local_pair(i, _):
        gbs, gcs, ds = [], [], []
        b_pair, c_pair = bt_ref[:, pair_lanes(i)], ct_ref[:, pair_lanes(i)]
        for k in range(2):
            c = i * 2 + k
            rows = pair_rows(i, k)
            spread_t = r2t_ref[256 * k : 256 * k + 256, :]
            bz = (dot(spread_t, b_pair, NT) * rmask).astype(BF16)
            cz = (dot(spread_t, c_pair, NT) * rmask).astype(BF16)
            bz_ref[rows, :] = bz
            cz_ref[rows, :] = cz
            xt, gt = xt_ref[rows, :], gt_ref[rows, :]
            bzt, czt = bzt_ref[c], czt_ref[c]
            mix = (dot(cz, bzt) * low_ref[...]).astype(BF16)
            mix_t = (dot(bz, czt) * lowt_ref[...]).astype(BF16)
            y = dot(mix, xt)
            z = dot(mix_t, gt)
            z_ref[rows, :] = z
            d = exact_fold(gt.astype(F32) * y, fold_in) + exact_fold(xt.astype(F32) * z, fold_out)
            ds.append(d * mask4)
            w = jnp.where(wmask_ref[...] > 0.5, dot(gt, xt, NT), 0.0).astype(BF16)
            gbs.append(dot(czt, w).astype(BF16))
            gcs.append(dot(bzt, w, NT).astype(BF16))
        hi, lo = split(jnp.concatenate(ds, axis=0))
        sums = dot(hi, suffix_plain, TN) + dot(lo, suffix_plain, TN)
        lg_ref[:, pair_lanes(i)] = sums[0:GH, 0:128]
        al_ref[:, pair_lanes(i)] = sums[GH : 2 * GH, 128:256]
        gbacc_ref[:, pair_lanes(i)] = dot(jnp.concatenate(gbs, axis=1), r2t_ref[...])
        gcacc_ref[:, pair_lanes(i)] = dot(jnp.concatenate(gcs, axis=1), r2t_ref[...])
        return 0

    lax.fori_loop(0, 1, local_pair, 0)

    settle(decall_ref, ss0, rs0)
    settle(ercv_ref, sse, rse)
    table = decall_ref[...].reshape(n, 128)
    for t in range(m):
        tile = me * m + t
        head = (tile // 16) * HEADS + (tile % 4) * 2 + over(sq1, DIM)
        decx_ref[t] = jnp.exp(dot(table, ones(sq0 == head), precision=HIGHEST))

    def scan_blocks(in_ref, out_ref, place):
        def lap(step, carry):
            k = place(step)
            out = []
            for t in range(m):
                out_ref[k, t] = carry[t].astype(BF16)
                out.append(decx_ref[t, pl.ds(k, 1), :] * carry[t] + in_ref[k, t].astype(F32))
            return tuple(out)

        lax.fori_loop(0, n, lap, tuple(jnp.zeros((16, 128), F32) for _ in range(m)))

    scan_blocks(ercv_ref, ssnd_ref, lambda k: k)
    srcv_ref[me] = ssnd_ref[me]
    copy_s = functools.partial(to_peer, lambda peer: ssnd_ref.at[peer], srcv_ref, sss, rss)
    each_peer(lambda i: copy_s(i).start())

    lax.fori_loop(1, 2, local_pair, 0)

    settle(frcv_ref, ssf, rsf)
    scan_blocks(frcv_ref, gsnd_ref, lambda k: n - 1 - k)
    grcv_ref[me] = gsnd_ref[me]
    copy_g = functools.partial(to_peer, lambda peer: gsnd_ref.at[peer], grcv_ref, ssg, rsg)
    each_peer(lambda i: copy_g(i).start())

    lax.fori_loop(2, PAIRS, local_pair, 0)

    settle(srcv_ref, sss, rss)
    from_slices(srcv_ref, s_ref)

    def s_pair(i, _):
        gcs, ds = [], []
        for k in range(2):
            c = i * 2 + k
            rows = pair_rows(i, k)
            advance(s_ref, e_ref, c, sp_ref)
            gt, sp = gt_ref[rows, :], sp_ref[c]
            out = dot(cz_ref[rows, :], sp)
            ds.append((dot((gt.astype(F32) * out).astype(BF16), fold_in) * mask4).astype(BF16))
            gcs.append((dot(sp, gt, NT) * gmask).astype(BF16))
        sums = dot(jnp.concatenate(ds, axis=0), suffix, TN)
        lg_ref[:, pair_lanes(i)] = lg_ref[:, pair_lanes(i)] + sums[0:GH]
        gcacc_ref[:, pair_lanes(i)] = gcacc_ref[:, pair_lanes(i)] + dot(jnp.concatenate(gcs, axis=1), r2t_ref[...])
        return 0

    lax.fori_loop(0, PAIRS, s_pair, 0)

    theirs = pl.ds(pl.multiple_of(other * 128, 128), 128)
    mine = pl.ds(pl.multiple_of(core * 128, 128), 128)

    def swap(j):
        return pltpu.make_async_remote_copy(
            src_ref=tsnd_ref.at[j], dst_ref=trcv_ref.at[j], send_sem=st4.at[j], recv_sem=rt4.at[j],
            device_id=(me, other), device_id_type=MESH,
        )

    tsnd_ref[1] = gcacc_ref[theirs, :].astype(BF16)
    swap(1).start()

    settle(grcv_ref, ssg, rsg)
    from_slices(grcv_ref, g2_ref)

    def gin_copy(i):
        part = pl.ds(i * 128, 128)
        return pltpu.make_async_copy(gin_ref.at[part], gin_hbm.at[part], out4.at[i])

    def g_cross(lap, _):
        i = PAIRS - 1 - lap
        ds = [None, None]
        for k in (1, 0):
            c = i * 2 + k
            rows = pair_rows(i, k)
            advance(g2_ref, f_ref, c, gp_ref)
            gp = gp_ref[c]
            through = sp_ref[c].astype(F32) * gp.astype(F32)
            for g in range(GROUPS):
                part = jnp.sum(through[DIM * g : DIM * g + DIM], axis=0, keepdims=True)
                th_ref[pl.ds(c * GROUPS + g, 1), :] = part
            back = dot(bz_ref[rows, :], gp)
            ds[k] = (dot((xt_ref[rows, :].astype(F32) * back).astype(BF16), fold_in) * mask4).astype(BF16)
            gin = (sx_ref[rows, :] * (z_ref[rows, :] + back)).astype(BF16)
            gin_ref[tokens_of(i, k)] = gin.reshape(CHUNK, GROUPS, WIDE)
        gin_copy(i).start()
        sums = dot(jnp.concatenate(ds, axis=0), before_plain, TN)
        lg_ref[:, pair_lanes(i)] = lg_ref[:, pair_lanes(i)] + sums[0:GH, 0:128]
        al_ref[:, pair_lanes(i)] = al_ref[:, pair_lanes(i)] + sums[0:GH, 128:256]
        return 0

    lax.fori_loop(0, PAIRS, g_cross, 0)

    th = dot(th_ref[...], ones(over(iota((WIDE, GH), 0), DIM) == within(iota((WIDE, GH), 1), HEADS)), precision=HIGHEST)
    th = jnp.where(within(iota((32, GH), 0), GROUPS) == over(iota((32, GH), 1), HEADS), th, 0.0)
    spread_th = ones(over(iota((32, TOK), 0), GROUPS) == over(iota((32, TOK), 1), CHUNK))
    log_grad = lg_ref[...] + dot(th, spread_th, TN, HIGHEST)
    late_rates = jnp.exp(column(alog_ref))
    late_u = dt_ref[...] + column(bias_ref)
    sig = 1.0 / (1.0 + jnp.exp(-late_u))
    graw = (al_ref[...] / step_ref[...] - late_rates * log_grad) * sig
    graw_ref[...] = graw
    alog_col = jnp.sum(log_grad * ld_ref[...], axis=1, keepdims=True)
    bias_col = jnp.sum(graw, axis=1, keepdims=True)
    pick = iota((GH, 128), 0) == iota((GH, 128), 1)
    alog_row = jnp.sum(jnp.where(pick, alog_col, 0.0), axis=0, keepdims=True)
    bias_row = jnp.sum(jnp.where(pick, bias_col, 0.0), axis=0, keepdims=True)
    tail_ref[...] = alog_row + pltpu.roll(bias_row, GH, 1)
    tailall_ref[me] = tail_ref[...]
    tail_copy = functools.partial(to_peer, lambda peer: tail_ref, tailall_ref, ss3, rs3)
    each_peer(lambda i: tail_copy(i).start())

    def b_pair(i, _):
        gbs = []
        for k in range(2):
            gbs.append((dot(gp_ref[i * 2 + k], xt_ref[pair_rows(i, k), :], NT) * gmask).astype(BF16))
        gbacc_ref[:, pair_lanes(i)] = gbacc_ref[:, pair_lanes(i)] + dot(jnp.concatenate(gbs, axis=1), r2t_ref[...])
        return 0

    lax.fori_loop(0, PAIRS, b_pair, 0)
    tsnd_ref[0] = gbacc_ref[theirs, :].astype(BF16)
    swap(0).start()
    swap(1).wait()
    gc_ref[...] = (gcacc_ref[mine, :] + trcv_ref[1].astype(F32)).astype(BF16)
    swap(0).wait()
    gb_ref[...] = (gbacc_ref[mine, :] + trcv_ref[0].astype(F32)).astype(BF16)
    for i in range(PAIRS):
        gin_copy(i).wait()

    settle(tailall_ref, ss3, rs3)
    sums = jnp.sum(tailall_ref[...].reshape(n, 128), axis=0, keepdims=True)
    sums = jnp.where(over(iota((8, 128), 1), HEADS) == iota((8, 128), 0), sums, 0.0)
    ends = dot(sums, ones(within(iota((128, HEADS), 0), HEADS) == iota((128, HEADS), 1)), precision=HIGHEST)
    galog_ref[...] = ends[0:4]
    gbias_ref[...] = ends[4:8]


def hand_over(*refs):
    big_in, big_out, held, ins, outs = refs[0], refs[6], refs[12], refs[13], refs[14]
    parts = [pl.ds(128 * i, 128) for i in range(PAIRS)]
    loads = [pltpu.make_async_copy(big_in.at[p], held.at[p], ins.at[i]) for i, p in enumerate(parts)]
    stores = [pltpu.make_async_copy(held.at[p], big_out.at[p], outs.at[i]) for i, p in enumerate(parts)]
    for load in loads:
        load.start()
    for j in range(1, 6):
        refs[6 + j][...] = refs[j][...]
    for load, store in zip(loads, stores):
        load.wait()
        store.start()
    for store in stores:
        store.wait()


def scratch(n):
    m = TILES // n
    dma = pltpu.SemaphoreType.DMA
    vm = pltpu.VMEM
    slices = (n, m, 16, 128)
    return [
        vm((TOK, GROUPS, WIDE), BF16), vm((TOK, GROUPS, WIDE), BF16), vm((TOK, GROUPS, WIDE), BF16),
        vm((TOK, 128), BF16), vm((2048, 128), BF16), vm((2048, WIDE), F32), vm((2048, WIDE), BF16), vm((2048, WIDE), BF16),
        vm((CHUNKS, 256, 256), BF16), vm((CHUNKS, 256, 256), BF16), vm((2048, 256), BF16), vm((2048, 256), BF16),
        vm((CHUNKS, 256, WIDE), F32), vm((CHUNKS, 256, WIDE), F32), vm((32, WIDE), F32),
        vm((256, WIDE), F32), vm((256, WIDE), F32), vm((CHUNKS, 256, WIDE), BF16), vm((CHUNKS, 256, WIDE), BF16),
        vm((2048, WIDE), F32), vm((GH, TOK), F32), vm((GH, TOK), F32), vm((256, TOK), F32), vm((256, TOK), F32),
        vm((32, WIDE), F32), vm((GH, TOK), F32), vm((GH, TOK), F32),
        vm((128, 512), BF16), vm((512, 128), BF16), vm((ROWS, ROWS), F32), vm((ROWS, ROWS), F32), vm((ROWS, ROWS), F32),
        vm((1, 128), F32), vm((n, 1, 128), F32), vm((m, n, 128), F32),
        vm(slices, BF16), vm(slices, BF16), vm(slices, BF16), vm(slices, BF16),
        vm(slices, BF16), vm(slices, BF16), vm(slices, BF16), vm(slices, BF16),
        vm((2, 128, TOK), BF16), vm((2, 128, TOK), BF16), vm((1, 128), F32), vm((n, 1, 128), F32),
        dma, dma, dma, dma, dma, dma, dma, dma, dma, dma, dma, dma, dma((2,)), dma((2,)), dma((2,)), dma((PAIRS,)),
    ]


def solution(mesh):
    n = mesh.shape["ctx"]

    def body(inputs, grad_out, dt_raw, dt_bias, a_log, b_proj, c_proj):
        bt = jnp.transpose(b_proj, (1, 2, 0)).reshape(GROUPS * DIM, TOK)
        ct = jnp.transpose(c_proj, (1, 2, 0)).reshape(GROUPS * DIM, TOK)
        vmem = pl.BlockSpec(memory_space=pltpu.VMEM)
        hbm = pl.BlockSpec(memory_space=pl.ANY)
        shapes = [
            jax.ShapeDtypeStruct((TOK, GROUPS, WIDE), BF16),
            jax.ShapeDtypeStruct((GH, TOK), F32),
            jax.ShapeDtypeStruct((GROUPS, HEADS), F32),
            jax.ShapeDtypeStruct((GROUPS, HEADS), F32),
            jax.ShapeDtypeStruct((128, TOK), BF16),
            jax.ShapeDtypeStruct((128, TOK), BF16),
        ]
        results = pl.pallas_call(
            functools.partial(kernel, n),
            out_shape=shapes,
            in_specs=[hbm] * 2 + [vmem] * 5,
            out_specs=[hbm] + [vmem] * 5,
            scratch_shapes=scratch(n),
            compiler_params=pltpu.CompilerParams(
                collective_id=0, has_side_effects=True, vmem_limit_bytes=58 * 2**20
            ),
        )(inputs, grad_out, dt_raw.reshape(GH, TOK), dt_bias, a_log, bt, ct)
        gin, graw, galog, gbias, gb, gc = pl.pallas_call(
            hand_over,
            out_shape=shapes,
            in_specs=[hbm] + [vmem] * 5,
            out_specs=[hbm] + [vmem] * 5,
            scratch_shapes=[
                pltpu.VMEM((TOK, GROUPS, WIDE), BF16), pltpu.SemaphoreType.DMA((PAIRS,)), pltpu.SemaphoreType.DMA((PAIRS,)),
            ],
            compiler_params=pltpu.CompilerParams(vmem_limit_bytes=58 * 2**20),
        )(*results)
        graw = graw.reshape(GROUPS, HEADS, TOK)
        gb = jnp.transpose(gb.reshape(2, DIM, TOK), (2, 0, 1))
        gc = jnp.transpose(gc.reshape(2, DIM, TOK), (2, 0, 1))
        return gin, graw, galog, gbias, gb, gc

    in_specs = (
        P("ctx", None, "tp"),
        P("ctx", None, "tp"),
        P(None, "tp", "ctx"),
        P(None, "tp"),
        P(None, "tp"),
        P("ctx", None, None),
        P("ctx", None, None),
    )
    out_specs = (
        P("ctx", None, "tp"),
        P(None, "tp", "ctx"),
        P(None, "tp"),
        P(None, "tp"),
        P("ctx", "tp", None),
        P("ctx", "tp", None),
    )
    return jax.shard_map(body, mesh=mesh, in_specs=in_specs, out_specs=out_specs, check_vma=False)
```

time: 69.6 us -> 51.3 us (0.74)
  Pallas kernels: 61.9 us -> 50.5 us
  local copies, waits for them, and re-layouts: 6.79 us -> 0 us
    pallas_call x1 -> x2, Pallas kernels: 61.9 us -> 50.5 us  [the longest x1 46.3 us: body(): pl.pallas_call(functools.partial(kernel, n), out_shape=shapes, in_specs=[...]
    unnamed x16 -> x0, local copies, waits for them, and re-layouts: 6.79 us -> none
where the time goes in v2:
time: 51.3 us; the launch traced here: 51.1 us
  Pallas kernels  50.5 us (98%)
  between operations  0.64 us (1%)
    pallas_call x1, Pallas kernels, body(): pl.pallas_call(functools.partial(kernel, n), out_shape=shapes, in_specs=[...  46.3 us
    pallas_call x1, Pallas kernels, body(): pl.pallas_call(hand_over, out_shape=shapes, in_specs=[hbm] + [vmem] * 5,...  4.16 us

profile of v2, /device:TPU:0, one launch (start us, length us, event | category | flops | bytes accessed | tf_op | source)
XLA Modules:
  0.0 51.1 jit_solution(6437093626950694107)
XLA Ops:
  0.6 46.3 %shard_map.118 = (bf16[512,4,512]{2,1,0:T(4,128)(2,1)}, f32[32,512]{1,0:T(8,128)}, f32[4,8]{1,0:T(4,128)}, f32[4,8]{1,0:T(4,128)}, bf16[128,512]{1,0:T(8,128)(2,1)}, /*index=5*/bf16[128,512]{1,0:T(8,128)(2,1)}) custom-call(bf16[512,4,512]{2,1,0:T(4,128)(2,1)} %x_hbm.1, bf16[512,4,512]{2,1,0:T(4,128)(2,1)} %g_hbm.1, f32[32,512]{1,0:T(8,128)} %bitcast.16, ...), custom_call_target="tpu_custom_call" | custom-call | tf_op jit(solution)/shard_map/pallas_call | solution.py:486
  47.0 4.2 %shard_map.119 = (bf16[512,4,512]{2,1,0:T(4,128)(2,1)}, f32[32,512]{1,0:T(8,128)}, f32[4,8]{1,0:T(4,128)}, f32[4,8]{1,0:T(4,128)}, bf16[128,512]{1,0:T(8,128)(2,1)}, /*index=5*/bf16[128,512]{1,0:T(8,128)(2,1)}) custom-call(bf16[512,4,512]{2,1,0:T(4,128)(2,1)} %get-tuple-element.18.refs_0_, f32[32,512]{1,0:T(8,128)} %get-tuple-element.19.refs_1_, ...), custom_call_target="tpu_custom_call" | custom-call | tf_op jit(solution)/shard_map/pallas_call | solution.py:496

commit v3 on v2

--- a/solution.py
+++ b/solution.py
@@ -7,7 +7,6 @@
 from jax.experimental.pallas import tpu as pltpu
 from jax.sharding import PartitionSpec as P
 
-HIGHEST = lax.Precision.HIGHEST
 F32 = jnp.float32
 BF16 = jnp.bfloat16
 MESH = pl.DeviceIdType.MESH
@@ -41,23 +40,41 @@
     return jnp.where(condition, 1.0, 0.0).astype(kind)
 
 
-def dot(a, b, contract=((1,), (0,)), precision=None):
-    return lax.dot_general(a, b, (contract, ((), ())), preferred_element_type=F32, precision=precision)
+def dot(a, b, contract=((1,), (0,))):
+    return lax.dot_general(a, b, (contract, ((), ())), preferred_element_type=F32)
 
 
 NT = ((1,), (1,))
 TN = ((0,), (0,))
 
 
+def thirds(value):
+    high = value.astype(BF16).astype(F32)
+    middle = (value - high).astype(BF16).astype(F32)
+    return jnp.concatenate([high, middle, value - high - middle], axis=0).astype(BF16)
+
+
+def add_thirds(value):
+    rows = value.shape[0] // 3
+    return value[:rows] + value[rows : 2 * rows] + value[2 * rows :]
+
+
+def far_first(n):
+    if n != 64:
+        return range(1, n)
+    steps = [(i // 16, i // 4 % 4, i % 4) for i in range(1, n)]
+    return sorted(steps, key=lambda step: -sum(min(way, 4 - way) for way in step))
+
+
 def kernel(
     n, x_hbm, g_hbm, dt_ref, bias_ref, alog_ref, bt_ref, ct_ref,
-    gin_hbm, graw_ref, galog_ref, gbias_ref, gb_ref, gc_ref,
-    x_ref, g_ref, gin_ref, st_ref, spread_ref, sx_ref, xt_ref, gt_ref, bzt_ref, czt_ref, bz_ref, cz_ref,
-    e_ref, f_ref, mul_ref, s_ref, g2_ref, sp_ref, gp_ref, z_ref, lg_ref, al_ref, gbacc_ref, gcacc_ref, th_ref,
+    gin_ref, graw_ref, galog_ref, gbias_ref, gb_ref, gc_ref,
+    x_ref, g_ref, st_ref, spread_ref, sx_ref, xt_ref, gt_ref, bzt_ref, czt_ref, bz_ref, cz_ref,
+    e_ref, f_ref, mul_ref, s_ref, g2_ref, sp_ref, gp_ref, z_ref, wb_ref, wc_ref, lg_ref, al_ref, gbacc_ref, gcacc_ref, th_ref,
     step_ref, ld_ref, r2_ref, r2t_ref, low_ref, lowt_ref, wmask_ref,
     decsrc_ref, decall_ref, decx_ref, esnd_ref, ercv_ref, fsnd_ref, frcv_ref, ssnd_ref, srcv_ref, gsnd_ref, grcv_ref,
     tsnd_ref, trcv_ref, tail_ref, tailall_ref,
-    ss0, rs0, sse, rse, ssf, rsf, sss, rss, ssg, rsg, ss3, rs3, st4, rt4, ld4, out4,
+    ss0, rs0, sse, rse, ssf, rsf, sss, rss, ssg, rsg, ss3, rs3, st4, rt4, ld4,
 ):
     m = TILES // n
     me = lax.axis_index("ctx")
@@ -77,8 +94,7 @@
     lax.fori_loop(1, n, greet, 0)
     pl.semaphore_signal(barrier, inc=1, device_id=(me, other), device_id_type=MESH)
 
-    def to_peer(src, dst, ssem, rsem, i):
-        peer = lax.rem(me + i, n)
+    def to_peer(src, dst, ssem, rsem, peer):
         return pltpu.make_async_remote_copy(
             src_ref=src(peer), dst_ref=dst.at[me], send_sem=ssem, recv_sem=rsem,
             device_id=(peer, core), device_id_type=MESH,
@@ -92,11 +108,12 @@
         ).wait()
 
     def each_peer(action):
-        def lap(i, _):
-            action(i)
-            return 0
-
-        lax.fori_loop(1, n, lap, 0)
+        for offset in far_first(n):
+            if n == 64:
+                spots = [lax.rem(lax.div(me, size) + step, 4) * size for size, step in zip((16, 4, 1), offset)]
+                action(spots[0] + spots[1] + spots[2])
+            else:
+                action(lax.rem(me + offset, n))
 
     diag = iota((HEADS, HEADS), 0) == iota((HEADS, HEADS), 1)
 
@@ -113,16 +130,11 @@
     ld_ref[...] = ld
     sq0, sq1 = iota((128, 128), 0), iota((128, 128), 1)
     same = over(sq0, CHUNK) == over(sq1, CHUNK)
-    tri = ones(same & (sq0 <= sq1))
-    block = ones(same)
-
-    def along_tokens(value, table):
-        return jnp.concatenate(
-            [dot(value[:, 128 * j : 128 * j + 128], table, precision=HIGHEST) for j in range(TOK // 128)], axis=1
-        )
-
-    cum = along_tokens(ld, tri)
-    half = along_tokens(ld, block) * 0.5
+    within_chunk = jnp.concatenate([ones(same & (sq0 <= sq1), BF16), ones(same, BF16)], axis=1)
+    four = jnp.concatenate([ld[:, 128 * j : 128 * j + 128] for j in range(TOK // 128)], axis=0)
+    sums = add_thirds(dot(thirds(four), within_chunk))
+    cum = jnp.concatenate([sums[GH * j : GH * j + GH, 0:128] for j in range(TOK // 128)], axis=1)
+    half = jnp.concatenate([sums[GH * j : GH * j + GH, 128:256] for j in range(TOK // 128)], axis=1) * 0.5
     sg = jnp.exp(cum - half)
     sx = step * jnp.exp(half - cum)
     sg_hi = sg.astype(BF16).astype(F32)
@@ -136,11 +148,11 @@
     decsrc_ref[...] = row
     decall_ref[me] = decsrc_ref[...]
 
-    first = ones(iota((TOK, CHUNKS * GROUPS), 0) == over(iota((TOK, CHUNKS * GROUPS), 1), GROUPS) * CHUNK)
-    half8 = dot(half, first, precision=HIGHEST)
+    chunk_of = ones(over(iota((TOK, CHUNKS * GROUPS), 0), CHUNK) == over(iota((TOK, CHUNKS * GROUPS), 1), GROUPS), BF16)
+    half8 = add_thirds(dot(thirds(ld), chunk_of)) * 0.5
     half8 = jnp.where(over(iota((GH, 32), 0), HEADS) == within(iota((GH, 32), 1), GROUPS), half8, 0.0)
-    by_head = ones(within(iota((GH, WIDE), 0), HEADS) == over(iota((GH, WIDE), 1), DIM))
-    mul_ref[...] = jnp.exp(dot(half8, by_head, TN, HIGHEST))
+    by_head = ones(within(iota((3 * GH, WIDE), 0), HEADS) == over(iota((3 * GH, WIDE), 1), DIM), BF16)
+    mul_ref[...] = jnp.exp(dot(thirds(half8), by_head, TN))
 
     r2_ref[...] = ones(iota((128, 512), 0) == over(iota((128, 512), 1), GROUPS), BF16)
     r2t_ref[...] = ones(iota((512, 128), 1) == over(iota((512, 128), 0), GROUPS), BF16)
@@ -160,6 +172,18 @@
     def tokens_of(i, k):
         return pl.ds(i * 128 + k * 64, 64)
 
+    def each_pair(step):
+        for i in range(PAIRS):
+            step(i, 0)
+
+    def twice(step):
+        def lap(j, _):
+            step(2 * j, 0)
+            step(2 * j + 1, 0)
+            return 0
+
+        lax.fori_loop(0, PAIRS // 2, lap, 0)
+
     def advance(state_ref, add_ref, c, low_out):
         for g in range(GROUPS):
             rows = slice(DIM * g, DIM * g + DIM)
@@ -167,7 +191,8 @@
             scaled = factor * state_ref[rows, :]
             if low_out is not None:
                 low_out[c, rows, :] = scaled.astype(BF16)
-            state_ref[rows, :] = factor * (scaled + add_ref[c, rows, :])
+            add = add_ref[c, rows, :] if low_out is not None else add_ref[rows]
+            state_ref[rows, :] = factor * (scaled + add)
 
     def to_slices(state_ref, out_ref):
         for t in range(TILES):
@@ -196,11 +221,12 @@
             xt_ref[rows, :] = xt
             bz_k = (bzt[:, 256 * k : 256 * k + 256] * gmask).astype(BF16)
             bzt_ref[c] = bz_k
-            e_ref[c] = dot(bz_k, xt)
-            advance(s_ref, e_ref, c, None)
-        return 0
-
-    lax.fori_loop(0, PAIRS, x_pair, 0)
+            e = dot(bz_k, xt)
+            e_ref[c] = e
+            advance(s_ref, e, c, None)
+        return 0
+
+    each_pair(x_pair)
     to_slices(s_ref, esnd_ref)
     ercv_ref[me] = esnd_ref[me]
     pl.semaphore_wait(barrier, n)
@@ -221,11 +247,12 @@
             gt_ref[rows, :] = gt
             cz_k = (czt[:, 256 * k : 256 * k + 256] * gmask).astype(BF16)
             czt_ref[c] = cz_k
-            f_ref[c] = dot(cz_k, gt)
-            advance(g2_ref, f_ref, c, None)
-        return 0
-
-    lax.fori_loop(0, PAIRS, g_pair, 0)
+            f = dot(cz_k, gt)
+            f_ref[c] = f
+            advance(g2_ref, f, c, None)
+        return 0
+
+    twice(g_pair)
     to_slices(g2_ref, fsnd_ref)
     frcv_ref[me] = fsnd_ref[me]
     copy_f = functools.partial(to_peer, lambda peer: fsnd_ref.at[peer], frcv_ref, ssf, rsf)
@@ -239,7 +266,7 @@
     es_row = over(iota((WIDE, 128), 0), DIM)
     es_lane = iota((WIDE, 128), 1)
     fold_in = ones((over(es_lane, GH) == 0) & (within(es_lane, HEADS) == es_row), BF16)
-    fold_out = ones((over(es_lane, GH) == 1) & (within(es_lane, HEADS) == es_row), BF16) - fold_in
+    fold_out = ones((over(es_lane, GH) == 1) & (within(es_lane, HEADS) == es_row), BF16)
     tr, tu = over(iota((512, 128), 0), GROUPS), iota((512, 128), 1)
     suffix = ones((tr >= tu) & (over(tr, CHUNK) == over(tu, CHUNK)), BF16)
     before = ones((tr < tu) & (over(tr, CHUNK) == over(tu, CHUNK)), BF16)
@@ -251,12 +278,8 @@
         hi = value.astype(BF16)
         return hi, (value - hi.astype(F32)).astype(BF16)
 
-    def exact_fold(value, table):
-        hi, lo = split(value)
-        return dot(hi, table) + dot(lo, table)
-
     def local_pair(i, _):
-        gbs, gcs, ds = [], [], []
+        ds = []
         b_pair, c_pair = bt_ref[:, pair_lanes(i)], ct_ref[:, pair_lanes(i)]
         for k in range(2):
             c = i * 2 + k
@@ -273,39 +296,43 @@
             y = dot(mix, xt)
             z = dot(mix_t, gt)
             z_ref[rows, :] = z
-            d = exact_fold(gt.astype(F32) * y, fold_in) + exact_fold(xt.astype(F32) * z, fold_out)
-            ds.append(d * mask4)
+            given = xt.astype(F32) * z
+            kept = gt.astype(F32) * y - given
+            hi, lo = split(kept)
+            ds.append((dot(hi, fold_in) + dot(lo, fold_in) + dot(given.astype(BF16), fold_out)) * mask4)
             w = jnp.where(wmask_ref[...] > 0.5, dot(gt, xt, NT), 0.0).astype(BF16)
-            gbs.append(dot(czt, w).astype(BF16))
-            gcs.append(dot(bzt, w, NT).astype(BF16))
+            wb_ref[c] = dot(czt, w).astype(BF16)
+            wc_ref[c] = dot(bzt, w, NT).astype(BF16)
         hi, lo = split(jnp.concatenate(ds, axis=0))
         sums = dot(hi, suffix_plain, TN) + dot(lo, suffix_plain, TN)
         lg_ref[:, pair_lanes(i)] = sums[0:GH, 0:128]
         al_ref[:, pair_lanes(i)] = sums[GH : 2 * GH, 128:256]
-        gbacc_ref[:, pair_lanes(i)] = dot(jnp.concatenate(gbs, axis=1), r2t_ref[...])
-        gcacc_ref[:, pair_lanes(i)] = dot(jnp.concatenate(gcs, axis=1), r2t_ref[...])
         return 0
 
     lax.fori_loop(0, 1, local_pair, 0)
 
     settle(decall_ref, ss0, rs0)
     settle(ercv_ref, sse, rse)
-    table = decall_ref[...].reshape(n, 128)
+    table = thirds(decall_ref[...].reshape(n, 128))
     for t in range(m):
         tile = me * m + t
         head = (tile // 16) * HEADS + (tile % 4) * 2 + over(sq1, DIM)
-        decx_ref[t] = jnp.exp(dot(table, ones(sq0 == head), precision=HIGHEST))
+        decx_ref[t] = jnp.exp(add_thirds(dot(table, ones(sq0 == head, BF16))))
 
     def scan_blocks(in_ref, out_ref, place):
+        width = 8 if n % 8 == 0 else 1
+
         def lap(step, carry):
-            k = place(step)
-            out = []
-            for t in range(m):
-                out_ref[k, t] = carry[t].astype(BF16)
-                out.append(decx_ref[t, pl.ds(k, 1), :] * carry[t] + in_ref[k, t].astype(F32))
-            return tuple(out)
-
-        lax.fori_loop(0, n, lap, tuple(jnp.zeros((16, 128), F32) for _ in range(m)))
+            for j in range(width):
+                k = place(step * width + j)
+                out = []
+                for t in range(m):
+                    out_ref[k, t] = carry[t].astype(BF16)
+                    out.append(decx_ref[t, pl.ds(k, 1), :] * carry[t] + in_ref[k, t].astype(F32))
+                carry = tuple(out)
+            return carry
+
+        lax.fori_loop(0, n // width, lap, tuple(jnp.zeros((16, 128), F32) for _ in range(m)))
 
     scan_blocks(ercv_ref, ssnd_ref, lambda k: k)
     srcv_ref[me] = ssnd_ref[me]
@@ -326,40 +353,30 @@
     from_slices(srcv_ref, s_ref)
 
     def s_pair(i, _):
-        gcs, ds = [], []
+        ds = []
         for k in range(2):
             c = i * 2 + k
             rows = pair_rows(i, k)
             advance(s_ref, e_ref, c, sp_ref)
             gt, sp = gt_ref[rows, :], sp_ref[c]
             out = dot(cz_ref[rows, :], sp)
-            ds.append((dot((gt.astype(F32) * out).astype(BF16), fold_in) * mask4).astype(BF16))
-            gcs.append((dot(sp, gt, NT) * gmask).astype(BF16))
-        sums = dot(jnp.concatenate(ds, axis=0), suffix, TN)
+            ds.append(dot((gt.astype(F32) * out).astype(BF16), fold_in) * mask4)
+        hi, lo = split(jnp.concatenate(ds, axis=0))
+        sums = dot(hi, suffix, TN) + dot(lo, suffix, TN)
         lg_ref[:, pair_lanes(i)] = lg_ref[:, pair_lanes(i)] + sums[0:GH]
-        gcacc_ref[:, pair_lanes(i)] = gcacc_ref[:, pair_lanes(i)] + dot(jnp.concatenate(gcs, axis=1), r2t_ref[...])
-        return 0
-
-    lax.fori_loop(0, PAIRS, s_pair, 0)
+        return 0
+
+    each_pair(s_pair)
 
     theirs = pl.ds(pl.multiple_of(other * 128, 128), 128)
     mine = pl.ds(pl.multiple_of(core * 128, 128), 128)
 
-    def swap(j):
-        return pltpu.make_async_remote_copy(
-            src_ref=tsnd_ref.at[j], dst_ref=trcv_ref.at[j], send_sem=st4.at[j], recv_sem=rt4.at[j],
-            device_id=(me, other), device_id_type=MESH,
-        )
-
-    tsnd_ref[1] = gcacc_ref[theirs, :].astype(BF16)
-    swap(1).start()
+    swap = pltpu.make_async_remote_copy(
+        src_ref=tsnd_ref, dst_ref=trcv_ref, send_sem=st4, recv_sem=rt4, device_id=(me, other), device_id_type=MESH
+    )
 
     settle(grcv_ref, ssg, rsg)
     from_slices(grcv_ref, g2_ref)
-
-    def gin_copy(i):
-        part = pl.ds(i * 128, 128)
-        return pltpu.make_async_copy(gin_ref.at[part], gin_hbm.at[part], out4.at[i])
 
     def g_cross(lap, _):
         i = PAIRS - 1 - lap
@@ -374,21 +391,21 @@
                 part = jnp.sum(through[DIM * g : DIM * g + DIM], axis=0, keepdims=True)
                 th_ref[pl.ds(c * GROUPS + g, 1), :] = part
             back = dot(bz_ref[rows, :], gp)
-            ds[k] = (dot((xt_ref[rows, :].astype(F32) * back).astype(BF16), fold_in) * mask4).astype(BF16)
-            gin = (sx_ref[rows, :] * (z_ref[rows, :] + back)).astype(BF16)
-            gin_ref[tokens_of(i, k)] = gin.reshape(CHUNK, GROUPS, WIDE)
-        gin_copy(i).start()
-        sums = dot(jnp.concatenate(ds, axis=0), before_plain, TN)
+            ds[k] = dot((xt_ref[rows, :].astype(F32) * back).astype(BF16), fold_in) * mask4
+            e_ref[c] = back
+        hi, lo = split(jnp.concatenate(ds, axis=0))
+        sums = dot(hi, before_plain, TN) + dot(lo, before_plain, TN)
         lg_ref[:, pair_lanes(i)] = lg_ref[:, pair_lanes(i)] + sums[0:GH, 0:128]
         al_ref[:, pair_lanes(i)] = al_ref[:, pair_lanes(i)] + sums[0:GH, 128:256]
         return 0
 
-    lax.fori_loop(0, PAIRS, g_cross, 0)
-
-    th = dot(th_ref[...], ones(over(iota((WIDE, GH), 0), DIM) == within(iota((WIDE, GH), 1), HEADS)), precision=HIGHEST)
+    each_pair(g_cross)
+
+    by_channel = ones(over(iota((WIDE, GH), 0), DIM) == within(iota((WIDE, GH), 1), HEADS), BF16)
+    th = add_thirds(dot(thirds(th_ref[...]), by_channel))
     th = jnp.where(within(iota((32, GH), 0), GROUPS) == over(iota((32, GH), 1), HEADS), th, 0.0)
-    spread_th = ones(over(iota((32, TOK), 0), GROUPS) == over(iota((32, TOK), 1), CHUNK))
-    log_grad = lg_ref[...] + dot(th, spread_th, TN, HIGHEST)
+    spread_th = ones(over(iota((96, TOK), 0) & 31, GROUPS) == over(iota((96, TOK), 1), CHUNK), BF16)
+    log_grad = lg_ref[...] + dot(thirds(th), spread_th, TN)
     late_rates = jnp.exp(column(alog_ref))
     late_u = dt_ref[...] + column(bias_ref)
     sig = 1.0 / (1.0 + jnp.exp(-late_u))
@@ -404,45 +421,49 @@
     tail_copy = functools.partial(to_peer, lambda peer: tail_ref, tailall_ref, ss3, rs3)
     each_peer(lambda i: tail_copy(i).start())
 
-    def b_pair(i, _):
-        gbs = []
+    def bc_pair(i, _):
+        gbs, gcs = [], []
         for k in range(2):
-            gbs.append((dot(gp_ref[i * 2 + k], xt_ref[pair_rows(i, k), :], NT) * gmask).astype(BF16))
-        gbacc_ref[:, pair_lanes(i)] = gbacc_ref[:, pair_lanes(i)] + dot(jnp.concatenate(gbs, axis=1), r2t_ref[...])
-        return 0
-
-    lax.fori_loop(0, PAIRS, b_pair, 0)
+            c = i * 2 + k
+            rows = pair_rows(i, k)
+            gbs.append((wb_ref[c].astype(F32) + dot(gp_ref[c], xt_ref[rows, :], NT) * gmask).astype(BF16))
+            gcs.append((wc_ref[c].astype(F32) + dot(sp_ref[c], gt_ref[rows, :], NT) * gmask).astype(BF16))
+        gbacc_ref[:, pair_lanes(i)] = dot(jnp.concatenate(gbs, axis=1), r2t_ref[...])
+        gcacc_ref[:, pair_lanes(i)] = dot(jnp.concatenate(gcs, axis=1), r2t_ref[...])
+        return 0
+
+    twice(bc_pair)
     tsnd_ref[0] = gbacc_ref[theirs, :].astype(BF16)
-    swap(0).start()
-    swap(1).wait()
+    tsnd_ref[1] = gcacc_ref[theirs, :].astype(BF16)
+    swap.start()
+
+    def gin_pair(i, _):
+        for k in range(2):
+            rows = pair_rows(i, k)
+            gin = (sx_ref[rows, :] * (z_ref[rows, :] + e_ref[i * 2 + k])).astype(BF16)
+            gin_ref[tokens_of(i, k)] = gin.reshape(CHUNK, GROUPS, WIDE)
+        return 0
+
+    lax.fori_loop(0, PAIRS, gin_pair, 0)
+    swap.wait()
+    gb_ref[...] = (gbacc_ref[mine, :] + trcv_ref[0].astype(F32)).astype(BF16)
     gc_ref[...] = (gcacc_ref[mine, :] + trcv_ref[1].astype(F32)).astype(BF16)
-    swap(0).wait()
-    gb_ref[...] = (gbacc_ref[mine, :] + trcv_ref[0].astype(F32)).astype(BF16)
-    for i in range(PAIRS):
-        gin_copy(i).wait()
 
     settle(tailall_ref, ss3, rs3)
     sums = jnp.sum(tailall_ref[...].reshape(n, 128), axis=0, keepdims=True)
     sums = jnp.where(over(iota((8, 128), 1), HEADS) == iota((8, 128), 0), sums, 0.0)
-    ends = dot(sums, ones(within(iota((128, HEADS), 0), HEADS) == iota((128, HEADS), 1)), precision=HIGHEST)
+    ends = add_thirds(dot(thirds(sums), ones(within(iota((128, HEADS), 0), HEADS) == iota((128, HEADS), 1), BF16)))
     galog_ref[...] = ends[0:4]
     gbias_ref[...] = ends[4:8]
 
 
 def hand_over(*refs):
-    big_in, big_out, held, ins, outs = refs[0], refs[6], refs[12], refs[13], refs[14]
-    parts = [pl.ds(128 * i, 128) for i in range(PAIRS)]
-    loads = [pltpu.make_async_copy(big_in.at[p], held.at[p], ins.at[i]) for i, p in enumerate(parts)]
-    stores = [pltpu.make_async_copy(held.at[p], big_out.at[p], outs.at[i]) for i, p in enumerate(parts)]
-    for load in loads:
-        load.start()
-    for j in range(1, 6):
-        refs[6 + j][...] = refs[j][...]
-    for load, store in zip(loads, stores):
-        load.wait()
-        store.start()
-    for store in stores:
-        store.wait()
+    ins, outs, sems = refs[:6], refs[6:12], refs[12]
+    copies = [pltpu.make_async_copy(a, b, sems.at[j]) for j, (a, b) in enumerate(zip(ins, outs))]
+    for copy in copies:
+        copy.start()
+    for copy in copies:
+        copy.wait()
 
 
 def scratch(n):
@@ -451,19 +472,20 @@
     vm = pltpu.VMEM
     slices = (n, m, 16, 128)
     return [
-        vm((TOK, GROUPS, WIDE), BF16), vm((TOK, GROUPS, WIDE), BF16), vm((TOK, GROUPS, WIDE), BF16),
+        vm((TOK, GROUPS, WIDE), BF16), vm((TOK, GROUPS, WIDE), BF16),
         vm((TOK, 128), BF16), vm((2048, 128), BF16), vm((2048, WIDE), F32), vm((2048, WIDE), BF16), vm((2048, WIDE), BF16),
         vm((CHUNKS, 256, 256), BF16), vm((CHUNKS, 256, 256), BF16), vm((2048, 256), BF16), vm((2048, 256), BF16),
         vm((CHUNKS, 256, WIDE), F32), vm((CHUNKS, 256, WIDE), F32), vm((32, WIDE), F32),
         vm((256, WIDE), F32), vm((256, WIDE), F32), vm((CHUNKS, 256, WIDE), BF16), vm((CHUNKS, 256, WIDE), BF16),
-        vm((2048, WIDE), F32), vm((GH, TOK), F32), vm((GH, TOK), F32), vm((256, TOK), F32), vm((256, TOK), F32),
+        vm((2048, WIDE), F32), vm((CHUNKS, 256, 256), BF16), vm((CHUNKS, 256, 256), BF16),
+        vm((GH, TOK), F32), vm((GH, TOK), F32), vm((256, TOK), F32), vm((256, TOK), F32),
         vm((32, WIDE), F32), vm((GH, TOK), F32), vm((GH, TOK), F32),
         vm((128, 512), BF16), vm((512, 128), BF16), vm((ROWS, ROWS), F32), vm((ROWS, ROWS), F32), vm((ROWS, ROWS), F32),
         vm((1, 128), F32), vm((n, 1, 128), F32), vm((m, n, 128), F32),
         vm(slices, BF16), vm(slices, BF16), vm(slices, BF16), vm(slices, BF16),
         vm(slices, BF16), vm(slices, BF16), vm(slices, BF16), vm(slices, BF16),
         vm((2, 128, TOK), BF16), vm((2, 128, TOK), BF16), vm((1, 128), F32), vm((n, 1, 128), F32),
-        dma, dma, dma, dma, dma, dma, dma, dma, dma, dma, dma, dma, dma((2,)), dma((2,)), dma((2,)), dma((PAIRS,)),
+        dma, dma, dma, dma, dma, dma, dma, dma, dma, dma, dma, dma, dma, dma, dma((2,)),
     ]
 
 
@@ -485,23 +507,21 @@
         ]
         results = pl.pallas_call(
             functools.partial(kernel, n),
-            out_shape=shapes,
+            out_shape=[pltpu.VMEM(shape.shape, shape.dtype) for shape in shapes],
             in_specs=[hbm] * 2 + [vmem] * 5,
-            out_specs=[hbm] + [vmem] * 5,
+            out_specs=[vmem] * 6,
             scratch_shapes=scratch(n),
             compiler_params=pltpu.CompilerParams(
-                collective_id=0, has_side_effects=True, vmem_limit_bytes=58 * 2**20
+                collective_id=0, has_side_effects=True, vmem_limit_bytes=56 * 2**20
             ),
         )(inputs, grad_out, dt_raw.reshape(GH, TOK), dt_bias, a_log, bt, ct)
         gin, graw, galog, gbias, gb, gc = pl.pallas_call(
             hand_over,
             out_shape=shapes,
-            in_specs=[hbm] + [vmem] * 5,
-            out_specs=[hbm] + [vmem] * 5,
-            scratch_shapes=[
-                pltpu.VMEM((TOK, GROUPS, WIDE), BF16), pltpu.SemaphoreType.DMA((PAIRS,)), pltpu.SemaphoreType.DMA((PAIRS,)),
-            ],
-            compiler_params=pltpu.CompilerParams(vmem_limit_bytes=58 * 2**20),
+            in_specs=[vmem] * 6,
+            out_specs=[hbm] * 6,
+            scratch_shapes=[pltpu.SemaphoreType.DMA((6,))],
+            compiler_params=pltpu.CompilerParams(vmem_limit_bytes=4 * 2**20),
         )(*results)
         graw = graw.reshape(GROUPS, HEADS, TOK)
         gb = jnp.transpose(gb.reshape(2, DIM, TOK), (2, 0, 1))

time: 51.3 us -> 41.8 us (0.81)
  Pallas kernels: 50.5 us -> 40.9 us
    pallas_call x2, Pallas kernels: 50.5 us -> 40.9 us  [the longest x1 39.4 us: body(): pl.pallas_call(functools.partial(kernel, n), out_shape=[pltpu.VMEM(shape....]
where the time goes in v3:
time: 41.8 us; the launch traced here: 41.7 us
  Pallas kernels  40.9 us (98%)
  between operations  0.8 us (2%)
    pallas_call x1, Pallas kernels, body(): pl.pallas_call(functools.partial(kernel, n), out_shape=[pltpu.VMEM(shape....  39.4 us
    pallas_call x1, Pallas kernels, body(): pl.pallas_call(hand_over, out_shape=shapes, in_specs=[vmem] * 6, out_spec...  1.47 us

profile of v3, /device:TPU:0, one launch (start us, length us, event | category | flops | bytes accessed | tf_op | source)
XLA Modules:
  0.0 41.7 jit_solution(8769479206378802766)
XLA Ops:
  0.6 39.4 %shard_map.118 = (bf16[512,4,512]{2,1,0:T(4,128)(2,1)S(1)}, f32[32,512]{1,0:T(8,128)S(1)}, f32[4,8]{1,0:T(4,128)S(1)}, f32[4,8]{1,0:T(4,128)S(1)}, bf16[128,512]...) custom-call(bf16[512,4,512]{2,1,0:T(4,128)(2,1)} %x_hbm.1, bf16[512,4,512]{2,1,0:T(4,128)(2,1)} %g_hbm.1, ...), custom_call_target="tpu_custom_call" | custom-call | tf_op jit(solution)/shard_map/pallas_call | solution.py:508
  40.1 1.5 %shard_map.119 = (bf16[512,4,512]{2,1,0:T(4,128)(2,1)}, f32[32,512]{1,0:T(8,128)}, f32[4,8]{1,0:T(4,128)}, f32[4,8]{1,0:T(4,128)}, bf16[128,512]{1,0:T(8,128)(2,1)}, /*index=5*/bf16[128,512]{1,0:T(8,128)(2,1)}) custom-call(bf16[512,4,512]{2,1,0:T(4,128)(2,1)S(1)} %get-tuple-element.18.refs_0_, f32[32,512]{1,0:T(8,128)S(1)} %get-tuple-element.19.refs_1_, ...), custom_call_target="tpu_custom_call" | custom-call | tf_op jit(solution)/shard_map/pallas_call | solution.py:518

commit v4 on v3

--- a/solution.py
+++ b/solution.py
@@ -67,9 +67,9 @@
 
 
 def kernel(
-    n, x_hbm, g_hbm, dt_ref, bias_ref, alog_ref, bt_ref, ct_ref,
+    n, x_hbm, g_hbm, dt_hbm, bias_hbm, alog_hbm, bt_hbm, ct_hbm,
     gin_ref, graw_ref, galog_ref, gbias_ref, gb_ref, gc_ref,
-    x_ref, g_ref, st_ref, spread_ref, sx_ref, xt_ref, gt_ref, bzt_ref, czt_ref, bz_ref, cz_ref,
+    x_ref, g_ref, dt_ref, bias_ref, alog_ref, bt_ref, ct_ref, st_ref, spread_ref, sx_ref, xt_ref, gt_ref, bzt_ref, czt_ref, bz_ref, cz_ref,
     e_ref, f_ref, mul_ref, s_ref, g2_ref, sp_ref, gp_ref, z_ref, wb_ref, wc_ref, lg_ref, al_ref, gbacc_ref, gcacc_ref, th_ref,
     step_ref, ld_ref, r2_ref, r2t_ref, low_ref, lowt_ref, wmask_ref,
     decsrc_ref, decall_ref, decx_ref, esnd_ref, ercv_ref, fsnd_ref, frcv_ref, ssnd_ref, srcv_ref, gsnd_ref, grcv_ref,
@@ -87,10 +87,10 @@
         pl.semaphore_signal(barrier, inc=1, device_id=(lax.rem(me + i, n), core), device_id_type=MESH)
         return 0
 
-    load_x = pltpu.make_async_copy(x_hbm, x_ref, ld4.at[0])
-    load_g = pltpu.make_async_copy(g_hbm, g_ref, ld4.at[1])
-    load_x.start()
-    load_g.start()
+    homes = (dt_hbm, dt_ref), (bias_hbm, bias_ref), (alog_hbm, alog_ref), (x_hbm, x_ref), (bt_hbm, bt_ref), (g_hbm, g_ref), (ct_hbm, ct_ref)
+    loads = [pltpu.make_async_copy(a, b, ld4.at[j]) for j, (a, b) in enumerate(homes)]
+    for load in loads:
+        load.start()
     lax.fori_loop(1, n, greet, 0)
     pl.semaphore_signal(barrier, inc=1, device_id=(me, other), device_id_type=MESH)
 
@@ -122,6 +122,8 @@
             [jnp.sum(jnp.where(diag, ref[g : g + 1, :], 0.0), axis=1, keepdims=True) for g in range(GROUPS)], axis=0
         )
 
+    for load in loads[:3]:
+        load.wait()
     rates = jnp.exp(column(alog_ref))
     u = dt_ref[...] + column(bias_ref)
     step = jnp.maximum(u, 0.0) + jnp.log1p(jnp.exp(-jnp.abs(u)))
@@ -206,7 +208,8 @@
 
     s_ref[...] = jnp.zeros_like(s_ref)
     g2_ref[...] = jnp.zeros_like(g2_ref)
-    load_x.wait()
+    loads[3].wait()
+    loads[4].wait()
 
     def x_pair(i, _):
         bzt = dot(bt_ref[:, pair_lanes(i)], r2_ref[...])
@@ -235,7 +238,8 @@
     copy_e = functools.partial(to_peer, lambda peer: esnd_ref.at[peer], ercv_ref, sse, rse)
     each_peer(lambda i: copy_e(i).start())
 
-    load_g.wait()
+    loads[5].wait()
+    loads[6].wait()
 
     def g_pair(lap, _):
         i = PAIRS - 1 - lap
@@ -252,7 +256,7 @@
             advance(g2_ref, f, c, None)
         return 0
 
-    twice(g_pair)
+    each_pair(g_pair)
     to_slices(g2_ref, fsnd_ref)
     frcv_ref[me] = fsnd_ref[me]
     copy_f = functools.partial(to_peer, lambda peer: fsnd_ref.at[peer], frcv_ref, ssf, rsf)
@@ -459,7 +463,9 @@
 
 def hand_over(*refs):
     ins, outs, sems = refs[:6], refs[6:12], refs[12]
-    copies = [pltpu.make_async_copy(a, b, sems.at[j]) for j, (a, b) in enumerate(zip(ins, outs))]
+    pairs = [(ins[0].at[pl.ds(128 * i, 128)], outs[0].at[pl.ds(128 * i, 128)]) for i in range(PAIRS)]
+    pairs += list(zip(ins[1:], outs[1:]))
+    copies = [pltpu.make_async_copy(a, b, sems.at[j]) for j, (a, b) in enumerate(pairs)]
     for copy in copies:
         copy.start()
     for copy in copies:
@@ -473,6 +479,7 @@
     slices = (n, m, 16, 128)
     return [
         vm((TOK, GROUPS, WIDE), BF16), vm((TOK, GROUPS, WIDE), BF16),
+        vm((GH, TOK), F32), vm((GROUPS, HEADS), F32), vm((GROUPS, HEADS), F32), vm((256, TOK), BF16), vm((256, TOK), BF16),
         vm((TOK, 128), BF16), vm((2048, 128), BF16), vm((2048, WIDE), F32), vm((2048, WIDE), BF16), vm((2048, WIDE), BF16),
         vm((CHUNKS, 256, 256), BF16), vm((CHUNKS, 256, 256), BF16), vm((2048, 256), BF16), vm((2048, 256), BF16),
         vm((CHUNKS, 256, WIDE), F32), vm((CHUNKS, 256, WIDE), F32), vm((32, WIDE), F32),
@@ -485,7 +492,7 @@
         vm(slices, BF16), vm(slices, BF16), vm(slices, BF16), vm(slices, BF16),
         vm(slices, BF16), vm(slices, BF16), vm(slices, BF16), vm(slices, BF16),
         vm((2, 128, TOK), BF16), vm((2, 128, TOK), BF16), vm((1, 128), F32), vm((n, 1, 128), F32),
-        dma, dma, dma, dma, dma, dma, dma, dma, dma, dma, dma, dma, dma, dma, dma((2,)),
+        dma, dma, dma, dma, dma, dma, dma, dma, dma, dma, dma, dma, dma, dma, dma((7,)),
     ]
 
 
@@ -508,7 +515,7 @@
         results = pl.pallas_call(
             functools.partial(kernel, n),
             out_shape=[pltpu.VMEM(shape.shape, shape.dtype) for shape in shapes],
-            in_specs=[hbm] * 2 + [vmem] * 5,
+            in_specs=[hbm] * 7,
             out_specs=[vmem] * 6,
             scratch_shapes=scratch(n),
             compiler_params=pltpu.CompilerParams(
@@ -520,7 +527,7 @@
             out_shape=shapes,
             in_specs=[vmem] * 6,
             out_specs=[hbm] * 6,
-            scratch_shapes=[pltpu.SemaphoreType.DMA((6,))],
+            scratch_shapes=[pltpu.SemaphoreType.DMA((PAIRS + 5,))],
             compiler_params=pltpu.CompilerParams(vmem_limit_bytes=4 * 2**20),
         )(*results)
         graw = graw.reshape(GROUPS, HEADS, TOK)

time: 41.8 us -> 41 us (0.981)
  Pallas kernels: 40.9 us -> 40 us
    pallas_call x1, Pallas kernels: 39.4 us -> 38.5 us  [body(): pl.pallas_call(functools.partial(kernel, n), out_shape=[pltpu.VMEM(shape....]
where the time goes in v4:
time: 41 us; the launch traced here: 40.8 us
  Pallas kernels  40 us (98%)
  between operations  0.8 us (2%)
    pallas_call x1, Pallas kernels, body(): pl.pallas_call(functools.partial(kernel, n), out_shape=[pltpu.VMEM(shape....  38.5 us
    pallas_call x1, Pallas kernels, body(): pl.pallas_call(hand_over, out_shape=shapes, in_specs=[vmem] * 6, out_spec...  1.5 us

profile of v4, /device:TPU:0, one launch (start us, length us, event | category | flops | bytes accessed | tf_op | source)
XLA Modules:
  0.0 40.8 jit_solution(17009472389166137387)
XLA Ops:
  0.6 38.5 %shard_map.118 = (bf16[512,4,512]{2,1,0:T(4,128)(2,1)S(1)}, f32[32,512]{1,0:T(8,128)S(1)}, f32[4,8]{1,0:T(4,128)S(1)}, f32[4,8]{1,0:T(4,128)S(1)}, bf16[128,512]...) custom-call(bf16[512,4,512]{2,1,0:T(4,128)(2,1)} %x_hbm.1, bf16[512,4,512]{2,1,0:T(4,128)(2,1)} %g_hbm.1, ...), custom_call_target="tpu_custom_call" | custom-call | tf_op jit(solution)/shard_map/pallas_call | solution.py:515
  39.2 1.5 %shard_map.119 = (bf16[512,4,512]{2,1,0:T(4,128)(2,1)}, f32[32,512]{1,0:T(8,128)}, f32[4,8]{1,0:T(4,128)}, f32[4,8]{1,0:T(4,128)}, bf16[128,512]{1,0:T(8,128)(2,1)}, /*index=5*/bf16[128,512]{1,0:T(8,128)(2,1)}) custom-call(bf16[512,4,512]{2,1,0:T(4,128)(2,1)S(1)} %get-tuple-element.18.refs_0_, f32[32,512]{1,0:T(8,128)S(1)} %get-tuple-element.19.refs_1_, ...), custom_call_target="tpu_custom_call" | custom-call | tf_op jit(solution)/shard_map/pallas_call | solution.py:525
